TPU v7x, 512 devices: a whole 4x4x16 slice. The times are simulated.
512 devices in a mesh: ctx: 128 (over z, x, core), dec: 4 (over y).
Axes of the slice: x: 4, y: 4, z: 16, core: 2. Of those that a mesh axis runs over, the one named last changes fastest.
Arguments:
- frames: bfloat16 [65536, 1280], P('ctx', 'dec'), may hold values from -20 to 20
- queries: bfloat16 [16384, 1280], P('ctx', 'dec'), may hold values from -128 to 128
- align_start: int32 [512], P('ctx'), may hold values from 0 to 2047, as said below
- align_end: int32 [512], P('ctx'), may hold values from 1 to 2048
- gain_conv: float32 [1280], P('dec'), may hold values from 0.25 to 1.75
- conv_kernel: float32 [31, 1280], P(None, 'dec'), may hold values from -1 to 1
- gain_attn: float32 [1280], P('dec'), may hold values from 0.25 to 1.75
- w_qkv: bfloat16 [1280, 3, 1280], P(None, None, 'dec'), may hold values from -3 to 3
- w_out: bfloat16 [1280, 1280], P(None, 'dec'), may hold values from -0.625 to 0.625
Outputs:
- encoded: bfloat16 [65536, 1280], P('ctx', 'dec')
- crossed: bfloat16 [16384, 1280], P('ctx', 'dec')
Inputs may be any that keep to these rules, and one draw needn't show every extreme that they name: Token blocks on ctx index c read only frame blocks of ctx indices c-1, c and c+1; align_end - align_start lies between 1 and 8 and equals 8 for the first token block of each ctx index.
All inputs are finite; a program needn't handle non-finite values.
Results may differ from a plain program's by a relative error of at most 0.029.
The roundings to bfloat16 on the way count: a program that leaves them out, or rounds other values in their place, can miss the bound.
Values may be sent and summed in bfloat16 or wider, within the bound.
No kernel may reach another device: no remote copies, remote signals or barrier semaphores. Data moves between devices by JAX's collectives and lax.ppermute only.
A program may use at most 64 MiB of HBM per device.

v0:
```python
import math

import jax
import jax.numpy as jnp
from jax import lax
from jax.sharding import PartitionSpec as P

HD = 64
D = 1280
WIN = 1024
FB = 32
SPAN_BLK = 8
TB = 32


def padded_2(cells, sides, width):
    for axis, dim in sides:
        count = lax.axis_size(axis)
        ends = count - 1
        head = lax.slice_in_dim(cells, 0, width, axis=dim)
        tail = lax.slice_in_dim(cells, cells.shape[dim] - width, cells.shape[dim], axis=dim)
        cells = jnp.concatenate(
            [
                lax.ppermute(tail, axis, [(i, (i + 1) % count) for i in range(ends)]),
                cells,
                lax.ppermute(head, axis, [((i + 1) % count, i) for i in range(ends)]),
            ],
            axis=dim,
        )
    return cells


def shifted(block, axis, distance):
    devices = range(lax.axis_size(axis))
    route = [(i - distance, i) for i in devices if i - distance in devices]
    return lax.ppermute(block, axis, route)


def masked_softmax(scores, keep):
    scores = jnp.where(keep, scores, -jnp.inf)
    peak = jnp.max(scores, axis=-1, keepdims=True)
    expo = jnp.exp(scores - peak)
    return expo / jnp.sum(expo, axis=-1, keepdims=True)


def cross_scores(kv_buffer, buffer_base, q_blocks, first_blocks, end_blocks):
    span = SPAN_BLK * FB
    buffer_len = kv_buffer.shape[1]
    width = min(span, buffer_len)
    blocks = q_blocks.shape[0]
    local_heads = q_blocks.shape[2]

    def take_window(first_blk):
        begin = jnp.clip(first_blk * FB - buffer_base, 0, buffer_len - width)
        return (lax.dynamic_slice_in_dim(kv_buffer, begin, width, 1), begin)

    windows, begins = jax.vmap(take_window)(first_blocks)
    k_win = windows[:, 0].reshape(blocks, width, local_heads, HD)
    v_win = windows[:, 1].reshape(blocks, width, local_heads, HD)
    scores = jnp.einsum(
        "bqhd,bkhd->bhqk", q_blocks, k_win, preferred_element_type=jnp.float32
    ) * HD ** (-0.5)
    kpos = buffer_base + begins[:, None] + jnp.arange(width, dtype=jnp.int32)[None, :]
    keep = (kpos >= first_blocks[:, None] * FB) & (kpos < end_blocks[:, None] * FB)
    return (scores, keep[:, None, None, :], v_win)


def local(frames, queries, align_start, align_end, gain_conv, conv_kernel, gain_attn, w_qkv, w_out):
    rows = frames.shape[0]
    local_width = frames.shape[1]
    local_heads = local_width // HD
    scale = HD ** (-0.5)
    x_float = frames.astype(jnp.float32)
    sumsq = lax.psum(jnp.sum(x_float * x_float, axis=1), "dec")
    normed = (x_float * lax.rsqrt(sumsq / D + 1e-06)[:, None] * gain_conv).astype(jnp.bfloat16)
    taps = conv_kernel.shape[0]
    half = (taps - 1) // 2
    padded = padded_2(normed, (("ctx", 0),), half)
    conv = jnp.zeros((rows, local_width), jnp.float32)
    for tap in range(taps):
        conv = conv + padded[tap : tap + rows].astype(jnp.float32) * conv_kernel[tap]
    resid = x_float + jax.nn.silu(conv)
    sumsq2 = lax.psum(jnp.sum(resid * resid, axis=1), "dec")
    normed2 = (resid * lax.rsqrt(sumsq2 / D + 1e-06)[:, None] * gain_attn).astype(jnp.bfloat16)
    w_flat = w_qkv.reshape(D, 3 * local_width)
    wrows = w_flat
    proj = jnp.dot(
        lax.all_gather(normed2, "dec", axis=1, tiled=True),
        wrows,
        preferred_element_type=jnp.float32,
    )
    q_own = proj[:, :local_width].astype(jnp.bfloat16)
    k_own = proj[:, local_width : 2 * local_width].astype(jnp.bfloat16)
    v_own = proj[:, 2 * local_width :].astype(jnp.bfloat16)
    key_val = jnp.stack([k_own, v_own], 0)
    key_rim = padded_2(key_val, (("ctx", 1),), rows)
    left_span = key_rim[:, :rows]
    reach = -(-WIN // rows)
    previous = shifted(key_val, "ctx", 2)
    earlier = [previous]
    window_kv = jnp.concatenate(earlier[::-1] + [left_span, key_val], axis=1)
    position = lax.axis_index("ctx")
    window_base = (position - reach) * rows
    q_rows = math.gcd(rows, 256)
    q_heads = q_own.reshape(rows, local_heads, HD)
    outputs = []
    for first in range(0, rows, q_rows):
        begin = first + reach * rows - WIN
        length = WIN + q_rows
        k_blk = window_kv[0, begin : begin + length].reshape(length, local_heads, HD)
        v_blk = window_kv[1, begin : begin + length].reshape(length, local_heads, HD)
        scores = (
            jnp.einsum(
                "qhd,khd->hqk",
                q_heads[first : first + q_rows],
                k_blk,
                preferred_element_type=jnp.float32,
            )
            * scale
        )
        qpos = position * rows + first + jnp.arange(q_rows, dtype=jnp.int32)
        kpos = window_base + begin + jnp.arange(length, dtype=jnp.int32)
        keep = (
            (kpos[None, :] <= qpos[:, None])
            & (kpos[None, :] > qpos[:, None] - WIN)
            & (kpos[None, :] >= 0)
        )
        probs = masked_softmax(scores, keep[None]).astype(jnp.bfloat16)
        out = jnp.einsum("hqk,khd->qhd", probs, v_blk, preferred_element_type=jnp.float32)
        outputs.append(out.reshape(q_rows, local_width).astype(jnp.bfloat16))
    attn = jnp.concatenate(outputs, axis=0)
    wrows = w_out
    mixed = jnp.dot(
        lax.all_gather(attn, "dec", axis=1, tiled=True), wrows, preferred_element_type=jnp.float32
    )
    encoded = (resid + mixed).astype(jnp.bfloat16)
    blocks = queries.shape[0] // TB
    q_blocks = queries.reshape(blocks, TB, local_heads, HD)
    scores, keep, v_win = cross_scores(
        key_rim, (position - 1) * rows, q_blocks, align_start, align_end
    )
    probs = masked_softmax(scores, keep).astype(jnp.bfloat16)
    out = jnp.einsum("bhqk,bkhd->bqhd", probs, v_win, preferred_element_type=jnp.float32)
    crossed = out.reshape(blocks * TB, local_width).astype(jnp.bfloat16)
    return (encoded, crossed)


def solution(mesh):
    placed = (
        P("ctx", "dec"),
        P("ctx", "dec"),
        P("ctx"),
        P("ctx"),
        P("dec"),
        P(None, "dec"),
        P("dec"),
        P(None, None, "dec"),
        P(None, "dec"),
    )
    return jax.shard_map(
        local,
        mesh=mesh,
        in_specs=placed,
        out_specs=(P("ctx", "dec"), P("ctx", "dec")),
        check_vma=False,
    )
```

profile of v0, /device:TPU:128, one launch (start us, length us, event | category | flops | bytes accessed | tf_op | source)
XLA Modules:
  0.0 178.4 jit_solution(7350062867338071864)
XLA Ops:
  7.2 1.2 fusion.25
  8.5 10.7 %psum.14 = f32[512]{0:T(512)S(1)} all-reduce(f32[512]{0:T(512)S(1)} %fusion.25), channel_id=1, replica_groups=mesh['ctx'=128,'dec'=4] {'dec'}, use_global_device_ids=true, to_apply=%region_1.0 | all-reduce | flops 512 | bytes 4096 | tf_op jit(solution)/shard_map/psum | solution.py:74
  19.2 1.1 fusion.27
  20.4 1.9 %collective-permute-start = (bf16[15,320]{0,1:T(8,128)(2,1)S(1)}, bf16[15,320]{0,1:T(8,128)(2,1)S(1)}, u32[]{:S(2)}, u32[]{:S(2)}) collective-permute-start(bf16[15,320]{0,1:T(8,128)(2,1)S(1)} %get-tuple-element.49), channel_id=1, source_target_pairs={{0,4},{4,8},{8,12},{12,16},{16,20},{20,24},{24,28},{28,32},{32,36}... | collective-permute-start | bytes 28808 | tf_op jit(solution)/shard_map/ppermute | solution.py:24
  22.3 7.0 %collective-permute-start.1 = (bf16[15,320]{0,1:T(8,128)(2,1)S(1)}, bf16[15,320]{0,1:T(8,128)(2,1)S(1)}, u32[]{:S(2)}, u32[]{:S(2)}) collective-permute-start(bf16[15,320]{0,1:T(8,128)(2,1)S(1)} %get-tuple-element.50), channel_id=1, source_target_pairs={{4,0},{8,4},{12,8},{16,12},{20,16},{24,20},{28,24},{32,28},{36,32}... | collective-permute-start | bytes 28808 | tf_op jit(solution)/shard_map/ppermute | solution.py:26
  29.3 1.2 slice_reduce_fusion.30
  31.6 7.7 %multiply_reduce_fusion = (f32[512]{0:T(512)S(1)}, f32[512,320]{0,1:T(8,128)S(1)}) fusion(f32[320]{0:T(512)S(1)} %get-tuple-element.33, bf16[15,320]{0,1:T(8,128)(2,1)S(1)} %collective-permute-done.1, bf16[512,320]{0,1:T(8,128)(2,1)S(1)} %fusion.27, f32[320]{0:T(512)S(1)} %get-tuple-element.34, f32[320]{0:T(512)S(1)} %get-tuple-element.5, ...), kind=kLoop, calls=%fused_computation.75 | loop fusion | flops 31129088 | bytes 1371648 | tf_op jit(solution)/shard_map/reduce_sum | solution.py:83
  39.3 7.7 %psum.15 = f32[512]{0:T(512)S(1)} all-reduce(f32[512]{0:T(512)S(1)} %get-tuple-element.35), channel_id=1, replica_groups=mesh['ctx'=128,'dec'=4] {'dec'}, use_global_device_ids=true, to_apply=%region_3.4 | all-reduce | flops 512 | bytes 4096 | tf_op jit(solution)/shard_map/psum | solution.py:83
  48.5 31.8 %all-gather.3.cloned.1.call-done = bf16[512,1280]{0,1:T(8,128)(2,1)} async-done(((bf16[512,320]{0,1:T(8,128)(2,1)}), bf16[512,1280]{0,1:T(8,128)(2,1)}) %all-gather.3.cloned.1.call-update) | async-done | bytes 1310736 | tf_op jit(solution)/shard_map/all_gather | solution.py:88
  80.2 2.7 %convolution_convert_fusion = bf16[512,960]{0,1:T(8,128)(2,1)S(1)} fusion(bf16[1280,960]{0,1:T(8,128)(2,1)S(1)} %bitcast.45, bf16[512,1280]{0,1:T(8,128)(2,1)} %all-gather.3.cloned.1.call-done), kind=kOutput, calls=%fused_computation.50 | convolution fusion | flops 1258782720 | bytes 4751360 | tf_op jit(solution)/shard_map/dot_general | solution.py:87
  83.1 3.4 %collective-permute-start.2 = (bf16[2,512,320]{1,2,0:T(8,128)(2,1)S(1)}, bf16[2,512,320]{1,2,0:T(8,128)(2,1)S(1)}, u32[]{:S(2)}, u32[]{:S(2)}) collective-permute-start(bf16[2,512,320]{1,2,0:T(8,128)(2,1)S(1)} %pad_maximum_fusion.1), channel_id=1, source_target_pairs={{0,8},{4,12},{8,16},{12,20},{16,24},{20,28},{24,32},{28,36},{32,40... | collective-permute-start | bytes 1966088 | tf_op jit(solution)/shard_map/ppermute | solution.py:36
  86.5 1.9 %collective-permute-start.3 = (bf16[2,512,320]{1,2,0:T(8,128)(2,1)S(1)}, bf16[2,512,320]{1,2,0:T(8,128)(2,1)S(1)}, u32[]{:S(2)}, u32[]{:S(2)}) collective-permute-start(bf16[2,512,320]{1,2,0:T(8,128)(2,1)S(1)} %pad_maximum_fusion.1), channel_id=1, source_target_pairs={{0,4},{4,8},{8,12},{12,16},{16,20},{20,24},{24,28},{28,32},{32,36}... | collective-permute-start | bytes 1966088 | tf_op jit(solution)/shard_map/ppermute | solution.py:24
  88.4 7.1 %collective-permute-start.4 = (bf16[2,512,320]{1,2,0:T(8,128)(2,1)S(1)}, bf16[2,512,320]{1,2,0:T(8,128)(2,1)S(1)}, u32[]{:S(2)}, u32[]{:S(2)}) collective-permute-start(bf16[2,512,320]{1,2,0:T(8,128)(2,1)S(1)} %pad_maximum_fusion.1), channel_id=1, source_target_pairs={{4,0},{8,4},{12,8},{16,12},{20,16},{24,20},{28,24},{32,28},{36,32}... | collective-permute-start | bytes 1966088 | tf_op jit(solution)/shard_map/ppermute | solution.py:26
  95.6 1.1 and_and_fusion
  97.4 8.6 %collective-permute-done.2 = bf16[2,512,320]{1,2,0:T(8,128)(2,1)S(1)} collective-permute-done((bf16[2,512,320]{1,2,0:T(8,128)(2,1)S(1)}, bf16[2,512,320]{1,2,0:T(8,128)(2,1)S(1)}, u32[]{:S(2)}, u32[]{:S(2)}) %collective-permute-start.2) | collective-permute-done | bytes 655392 | tf_op jit(solution)/shard_map/ppermute | solution.py:36
  106.0 4.6 %collective-permute-done.3 = bf16[2,512,320]{1,2,0:T(8,128)(2,1)S(1)} collective-permute-done((bf16[2,512,320]{1,2,0:T(8,128)(2,1)S(1)}, bf16[2,512,320]{1,2,0:T(8,128)(2,1)S(1)}, u32[]{:S(2)}, u32[]{:S(2)}) %collective-permute-start.3) | collective-permute-done | bytes 655392 | tf_op jit(solution)/shard_map/ppermute | solution.py:24
  110.6 1.4 pad_maximum_fusion
  112.0 1.7 fusion.76
  113.8 3.5 %fusion.81 = f32[5,256]{1,0:T(8,128)S(1)} fusion(pred[256,1280]{1,0:T(8,128)(4,1)S(1)} %and_and_fusion.1, bf16[256,5,64]{0,2,1:T(8,128)(2,1)} %bitcast.56, bf16[1280,5,64]{0,2,1:T(8,128)(2,1)} %bitcast.50), kind=kOutput, calls=%fused_computation.201 | convolution fusion | flops 216270080 | bytes 1315840 | tf_op jit(solution)/shard_map/sub | solution.py:42
  117.3 4.7 %fusion.19 = bf16[5,64,256]{2,1,0:T(8,128)(2,1)} fusion(bf16[1280,5,64]{0,2,1:T(8,128)(2,1)} %bitcast.52, f32[5,256]{1,0:T(8,128)S(1)} %fusion.81, pred[256,1280]{1,0:T(8,128)(4,1)S(1)} %and_and_fusion.1, bf16[256,5,64]{0,2,1:T(8,128)(2,1)} %bitcast.57, bf16[1280,5,64]{0,2,1:T(8,128)(2,1)} %bitcast.51), kind=kOutput, calls=%fused_computation.62 | convolution fusion | flops 427706880 | bytes 2298880 | tf_op jit(solution)/shard_map/hqk,khd->qhd/dot_general | solution.py:129
  122.0 3.6 %fusion.80 = f32[5,256]{1,0:T(8,128)S(1)} fusion(pred[256,1280]{1,0:T(8,128)(4,1)} %and_and_fusion, bf16[256,5,64]{0,2,1:T(8,128)(2,1)} %bitcast.54, bf16[1280,5,64]{0,2,1:T(8,128)(2,1)} %bitcast.47), kind=kOutput, calls=%fused_computation.200 | convolution fusion | flops 216270080 | bytes 1315840 | tf_op jit(solution)/shard_map/sub | solution.py:42
  125.7 4.8 %fusion.18 = bf16[5,64,256]{2,1,0:T(8,128)(2,1)} fusion(bf16[1280,5,64]{0,2,1:T(8,128)(2,1)} %bitcast.49, f32[5,256]{1,0:T(8,128)S(1)} %fusion.80, pred[256,1280]{1,0:T(8,128)(4,1)} %and_and_fusion, bf16[256,5,64]{0,2,1:T(8,128)(2,1)S(1)} %bitcast.55, bf16[1280,5,64]{0,2,1:T(8,128)(2,1)} %bitcast.48), kind=kOutput, calls=%fused_computation.61 | convolution fusion | flops 427706880 | bytes 2298880 | tf_op jit(solution)/shard_map/hqk,khd->qhd/dot_general | solution.py:129
  130.5 1.7 pad_maximum_fusion.4
  132.5 6.8 %copy.15 = bf16[2,1536,320]{2,0,1:T(2,128)(2,1)} copy(bf16[2,1536,320]{1,2,0:T(8,128)(2,1)} %get-tuple-element.43) | data formatting | bytes 3932160 | tf_op jit(solution)/shard_map/concatenate | solution.py:22
  139.2 6.7 %gather_fusion = bf16[4,2,256,320]{3,1,2,0:T(2,128)(2,1)} fusion(bf16[2,1536,320]{2,0,1:T(2,128)(2,1)} %copy.15, s32[4]{0:T(128)S(1)} %get-tuple-element.53), kind=kCustom, calls=%fused_computation | custom fusion | bytes 2621488 | tf_op jit(solution)/shard_map/vmap()/gather | solution.py:55
  145.9 5.7 %fusion.77 = (bf16[4,1,256,320]{3,1,2,0:T(2,128)(2,1)}, bf16[4,1,256,320]{3,1,2,0:T(2,128)(2,1)}) fusion(bf16[4,2,256,320]{3,1,2,0:T(2,128)(2,1)} %gather_fusion), kind=kLoop, calls=%fused_computation.197 | loop fusion | bytes 2621440 | tf_op jit(solution)/shard_map/slice | solution.py:58
  151.7 4.6 %copy.17 = bf16[4,1,256,320]{2,3,0,1:T(8,128)(2,1)} copy(bf16[4,1,256,320]{3,1,2,0:T(2,128)(2,1)} %get-tuple-element.41) | data formatting | bytes 1310720 | tf_op jit(solution)/shard_map/slice | solution.py:58
  156.3 4.6 %copy.16 = bf16[4,1,256,320]{2,3,0,1:T(8,128)(2,1)} copy(bf16[4,1,256,320]{3,1,2,0:T(2,128)(2,1)} %get-tuple-element.42) | data formatting | bytes 1310720 | tf_op jit(solution)/shard_map/slice | solution.py:59
  160.9 1.4 fusion.16
  163.4 3.3 %fusion.20 = bf16[4,32,5,64]{3,1,2,0:T(8,128)(2,1)} fusion(bf16[4,256,5,64]{1,3,2,0:T(8,128)(2,1)} %bitcast.53, f32[4,5,32]{2,1,0:T(8,128)S(1)} %fusion.82, f32[4,5,32,256]{3,2,1,0:T(8,128)} %copy-done.1), kind=kOutput, calls=%fused_computation.63 | convolution fusion | flops 21504896 | bytes 1395200 | tf_op jit(solution)/shard_map/bhqk,bkhd->bqhd/dot_general | solution.py:143
  166.7 1.1 copy.24
  168.7 2.9 %fusion.17 = bf16[512,320]{0,1:T(8,128)(2,1)} fusion(f32[512,320]{0,1:T(8,128)S(1)} %get-tuple-element.36, bf16[1280,320]{0,1:T(8,128)(2,1)} %param.17, bf16[512,1280]{0,1:T(8,128)(2,1)} %all-gather.5.cloned.1.call-done), kind=kOutput, calls=%fused_computation.59 | convolution fusion | flops 419758080 | bytes 3112960 | tf_op jit(solution)/shard_map/dot_general | solution.py:133
  (45 shorter events, 5.6 us)
Async XLA Ops:
  7.2 73.1 %copy-start = (bf16[1280,3,320]{0,2,1:T(8,128)(2,1)S(1)}, bf16[1280,3,320]{0,2,1:T(8,128)(2,1)}, u32[]{:S(2)}) copy-start(bf16[1280,3,320]{0,2,1:T(8,128)(2,1)} %param.16) | copy-start | bytes 7372804
  7.2 39.9 %copy-start.5 = (f32[320]{0:T(512)S(1)}, f32[320]{0:T(512)}, u32[]{:S(2)}) copy-start(f32[320]{0:T(512)} %param.15) | copy-start | bytes 3844
  7.2 73.0 %all-gather.3.cloned.1.call-start = ((), (), s32[]{:S(2)}) async-start(), calls=%async_computation | async-start | bytes 1638400 | tf_op jit(solution)/shard_map/all_gather | solution.py:88
  20.4 11.2 %collective-permute-start = (bf16[15,320]{0,1:T(8,128)(2,1)S(1)}, bf16[15,320]{0,1:T(8,128)(2,1)S(1)}, u32[]{:S(2)}, u32[]{:S(2)}) collective-permute-start(bf16[15,320]{0,1:T(8,128)(2,1)S(1)} %get-tuple-element.49), channel_id=1, source_target_pairs={{0,4},{4,8},{8,12},{12,16},{16,20},{20,24},{24,28},{28,32},{32,36}... | collective-permute-start | bytes 28808 | tf_op jit(solution)/shard_map/ppermute | solution.py:24
  22.3 9.3 %collective-permute-start.1 = (bf16[15,320]{0,1:T(8,128)(2,1)S(1)}, bf16[15,320]{0,1:T(8,128)(2,1)S(1)}, u32[]{:S(2)}, u32[]{:S(2)}) collective-permute-start(bf16[15,320]{0,1:T(8,128)(2,1)S(1)} %get-tuple-element.50), channel_id=1, source_target_pairs={{4,0},{8,4},{12,8},{16,12},{20,16},{24,20},{28,24},{32,28},{36,32}... | collective-permute-start | bytes 28808 | tf_op jit(solution)/shard_map/ppermute | solution.py:26
  47.9 120.8 %all-gather.5.cloned.1.call-start = ((), (), s32[]{:S(2)}) async-start(), calls=%async_computation.1 | async-start | bytes 1638400 | tf_op jit(solution)/shard_map/all_gather | solution.py:134
  83.1 22.9 %collective-permute-start.2 = (bf16[2,512,320]{1,2,0:T(8,128)(2,1)S(1)}, bf16[2,512,320]{1,2,0:T(8,128)(2,1)S(1)}, u32[]{:S(2)}, u32[]{:S(2)}) collective-permute-start(bf16[2,512,320]{1,2,0:T(8,128)(2,1)S(1)} %pad_maximum_fusion.1), channel_id=1, source_target_pairs={{0,8},{4,12},{8,16},{12,20},{16,24},{20,28},{24,32},{28,36},{32,40... | collective-permute-start | bytes 1966088 | tf_op jit(solution)/shard_map/ppermute | solution.py:36
  86.5 24.1 %collective-permute-start.3 = (bf16[2,512,320]{1,2,0:T(8,128)(2,1)S(1)}, bf16[2,512,320]{1,2,0:T(8,128)(2,1)S(1)}, u32[]{:S(2)}, u32[]{:S(2)}) collective-permute-start(bf16[2,512,320]{1,2,0:T(8,128)(2,1)S(1)} %pad_maximum_fusion.1), channel_id=1, source_target_pairs={{0,4},{4,8},{8,12},{12,16},{16,20},{20,24},{24,28},{28,32},{32,36}... | collective-permute-start | bytes 1966088 | tf_op jit(solution)/shard_map/ppermute | solution.py:24
  88.4 22.2 %collective-permute-start.4 = (bf16[2,512,320]{1,2,0:T(8,128)(2,1)S(1)}, bf16[2,512,320]{1,2,0:T(8,128)(2,1)S(1)}, u32[]{:S(2)}, u32[]{:S(2)}) collective-permute-start(bf16[2,512,320]{1,2,0:T(8,128)(2,1)S(1)} %pad_maximum_fusion.1), channel_id=1, source_target_pairs={{4,0},{8,4},{12,8},{16,12},{20,16},{24,20},{28,24},{32,28},{36,32}... | collective-permute-start | bytes 1966088 | tf_op jit(solution)/shard_map/ppermute | solution.py:26
  122.0 3.6 %copy-start.2 = (bf16[256,320]{0,1:T(8,128)(2,1)S(1)}, bf16[256,320]{0,1:T(8,128)(2,1)}, u32[]{:S(2)}) copy-start(bf16[256,320]{0,1:T(8,128)(2,1)} %get-tuple-element.46) | copy-start | bytes 491524
  125.6 4.9 %copy-start.3 = (bf16[5,64,256]{2,1,0:T(8,128)(2,1)S(1)}, bf16[5,64,256]{2,1,0:T(8,128)(2,1)}, u32[]{:S(2)}) copy-start(bf16[5,64,256]{2,1,0:T(8,128)(2,1)} %fusion.19) | copy-start | bytes 491524
  125.6 6.5 %copy-start.4 = (bf16[128,320]{0,1:T(8,128)(2,1)S(1)}, bf16[128,320]{0,1:T(8,128)(2,1)}, u32[]{:S(2)}) copy-start(bf16[128,320]{0,1:T(8,128)(2,1)} %param.10) | copy-start | bytes 245764
  125.7 6.7 %copy-start.7 = (s32[4]{0:T(128)S(1)}, s32[4]{0:T(128)}, u32[]{:S(2)}) copy-start(s32[4]{0:T(128)} %param.12) | copy-start | bytes 52
  125.7 6.7 %copy-start.6 = (s32[4]{0:T(128)S(1)}, s32[4]{0:T(128)}, u32[]{:S(2)}) copy-start(s32[4]{0:T(128)} %param.11) | copy-start | bytes 52
  162.3 0.8 copy-start.1
Sparse Core Ops, SparseCore 0:
  48.1 32.1 all-gather.2
  132.3 31.0 all-gather.4
where the time goes:
time: 180 us; the launch traced here: 178 us
  waiting for transfers between devices  45 us (25%)
  local copies, waits for them, and re-layouts  36.3 us (20%)
  matrix products  27 us (15%)
  starting transfers between devices  21.4 us (12%)
  blocking collectives  18.5 us (10%)
  other arithmetic  15.8 us (9%)
  between operations  14.3 us (8%)
    all_gather x1, waiting for transfers between devices, local(): lax.all_gather(normed2, 'dec', axis=1, tiled=True)  31.8 us
    ppermute x2, starting transfers between devices, padded_2(): lax.ppermute(head, axis, [((i + 1) % count, i) for i in range(ends)])  14.1 us
    psum x1, blocking collectives, local(): sumsq = lax.psum(jnp.sum(x_float * x_float, axis=1), 'dec')  10.7 us
    slice x2, local copies, waits for them, and re-layouts, cross_scores(): k_win = windows[:, 0].reshape(blocks, width, local_heads, HD)  10.3 us
    dot_general x2, matrix products, local(): jnp.einsum('hqk,khd->qhd', probs, v_blk, preferred_element_type=jnp.float32)  9.55 us
    ppermute x1, waiting for transfers between devices, shifted(): return lax.ppermute(block, axis, route)  8.57 us
    psum x1, blocking collectives, local(): sumsq2 = lax.psum(jnp.sum(resid * resid, axis=1), 'dec')  7.75 us
    reduce_sum x1, other arithmetic, local(): sumsq2 = lax.psum(jnp.sum(resid * resid, axis=1), 'dec')  7.71 us
  transfers between devices with their start and end apart: 7, of which 3 were waited for; matrix products, arithmetic and copies ran while one was open for 22% of the time, Pallas kernels for 0%

commit v1 on v0

v1 whole, which is shorter than its diff:
```python
import functools

import jax
import jax.numpy as jnp
from jax import lax
from jax.experimental import pallas as pl
from jax.experimental.pallas import tpu as pltpu
from jax.sharding import PartitionSpec as P

HD = 64
D = 1280
WIN = 1024
FB = 32
TB = 32
KW = 31
HALF = 15
EPS = 1e-06
SCALE = HD ** (-0.5)
LOG2E = 1.4426950408889634
FAR = 1e30
RIM = 16
LANES = 128

VMEM = pl.BlockSpec(memory_space=pltpu.VMEM)
SMEM = pl.BlockSpec(memory_space=pltpu.SMEM)
HBM = pl.BlockSpec(memory_space=pltpu.HBM)


def call(kernel, outs, smem, operands, scratch=(), hbm=0, mib=16, flops=0, nbytes=0, exps=0):
    specs = [SMEM] * smem + [VMEM] * (len(operands) - smem - hbm) + [HBM] * hbm
    return pl.pallas_call(
        kernel,
        out_shape=outs,
        in_specs=specs,
        out_specs=jax.tree.map(lambda _: VMEM, outs),
        scratch_shapes=list(scratch),
        compiler_params=pltpu.CompilerParams(vmem_limit_bytes=mib * 1024 * 1024),
        cost_estimate=pl.CostEstimate(flops=flops, bytes_accessed=nbytes, transcendentals=exps),
    )(*operands)


def rot(block, axis, distance):
    count = lax.axis_size(axis)
    return lax.ppermute(block, axis, [(i, (i + distance) % count) for i in range(count)])


def shifted(block, axis, distance):
    devices = range(lax.axis_size(axis))
    return lax.ppermute(block, axis, [(i, i + distance) for i in devices if i + distance in devices])


def pack_body(left_ref, right_ref, taps_ref, gain1_ref, gain2_ref, out_ref):
    out_ref[0:RIM, :] = left_ref[...].astype(jnp.float32)
    out_ref[RIM : 2 * RIM, :] = right_ref[...].astype(jnp.float32)
    out_ref[2 * RIM : 2 * RIM + KW, :] = taps_ref[...]
    out_ref[2 * RIM + KW : 2 * RIM + KW + 1, :] = gain1_ref[...]
    out_ref[2 * RIM + KW + 1 : 2 * RIM + KW + 2, :] = gain2_ref[...]
    out_ref[2 * RIM + KW + 2 :, :] = jnp.zeros((7, out_ref.shape[1]), jnp.float32)


def hold_body(in_ref, out_ref, sem):
    copy = pltpu.make_async_copy(in_ref, out_ref, sem)
    copy.start()
    copy.wait()


def place(dec, blocks, whole_ref, width):
    for offset, block in blocks:
        at = pl.multiple_of(lax.rem(dec + offset, 4) * width, width)
        whole_ref[pl.ds(at, width), :] = block[:width, :]


def rounded(value):
    return value.astype(jnp.bfloat16).astype(jnp.float32)


def front_body(
    dec_ref, own_ref, b1_ref, b2_ref, b3_ref, pay_ref, w_ref, q_ref, kv_ref, resid_ref,
    xall_ref, x_ref, pad_ref, scale_ref, square_ref, whole_ref, turned_ref, norm_ref,
):
    width, rows = own_ref.shape
    dec = dec_ref[0]
    place(dec, [(0, own_ref), (3, b1_ref), (2, b2_ref), (1, b3_ref)], xall_ref, width)
    tiles = D // LANES

    def gather_square(f, total):
        at = pl.ds(pl.multiple_of(f * LANES, LANES), LANES)
        x = xall_ref[at, :].astype(jnp.float32)
        return total + jnp.sum((x * x).reshape(LANES // 8, 8, rows), axis=0)

    total = lax.fori_loop(0, tiles, gather_square, jnp.zeros((8, rows), jnp.float32))
    scale = lax.rsqrt(jnp.sum(total, axis=0, keepdims=True) / D + EPS)
    scale_ref[...] = jnp.broadcast_to(scale, (LANES, rows)).T
    rims = pay_ref[0 : 2 * RIM, :]
    rim_scale = lax.rsqrt(jnp.sum(rims * rims, axis=1, keepdims=True) / D + EPS)
    square_ref[...] = jnp.zeros_like(square_ref)
    strip = 64

    def tile(f, carry):
        lanes = pl.ds(pl.multiple_of(f * LANES, LANES), LANES)
        gain = pay_ref[2 * RIM + KW : 2 * RIM + KW + 1, lanes]
        x_ref[...] = xall_ref[lanes, :].astype(jnp.float32).T
        rim = rounded(pay_ref[0 : 2 * RIM, lanes] * rim_scale * gain)
        pad_ref[0:RIM, :] = rim[:RIM]
        pad_ref[RIM + rows : 2 * RIM + rows, :] = rim[RIM:]
        pad_ref[RIM : RIM + rows, :] = rounded(x_ref[...] * scale_ref[...] * gain)
        for t in range(0, rows, strip):
            conv = None
            for b in range(8):
                moved = pad_ref[t + b + 1 : t + b + 1 + strip + 24, :]
                for a in range(4):
                    tap = 8 * a + b
                    if tap < KW:
                        k = pay_ref[2 * RIM + tap : 2 * RIM + tap + 1, lanes]
                        term = moved[8 * a : 8 * a + strip] * k
                        conv = term if conv is None else conv + term
            resid = x_ref[t : t + strip, :] + conv / (1.0 + jnp.exp(-conv))
            whole_ref[f, t : t + strip, :] = resid
            square_ref[t : t + strip, :] += resid * resid

        @pl.when((f * LANES < (dec + 1) * width) & ((f + 1) * LANES > dec * width))
        def _():
            turned_ref[lanes, :] = whole_ref[f].T

        return carry

    lax.fori_loop(0, tiles, tile, 0)
    resid_ref[...] = turned_ref[pl.ds(pl.multiple_of(dec * width, HD), width), :]
    scale2 = lax.rsqrt(jnp.sum(square_ref[...], axis=1, keepdims=True) / D + EPS)
    for f in range(tiles):
        lanes = slice(f * LANES, (f + 1) * LANES)
        gain = pay_ref[2 * RIM + KW + 1 : 2 * RIM + KW + 2, lanes]
        norm_ref[:, lanes] = (whole_ref[f] * scale2 * gain).astype(jnp.bfloat16)
    for third in (1, 2, 0):
        proj = lax.dot_general(
            w_ref[third * width : (third + 1) * width, :],
            norm_ref[...],
            (((1,), (1,)), ((), ())),
            preferred_element_type=jnp.float32,
        ).astype(jnp.bfloat16)
        if third == 0:
            q_ref[...] = proj * jnp.bfloat16(SCALE)
        else:
            kv_ref[(third - 1) * width : third * width, :] = proj


def tdot(left, right):
    return lax.dot_general(left, right, (((0,), (0,)), ((), ())), preferred_element_type=jnp.float32)


def self_body(pos_ref, q_ref, own_ref, left_ref, far_ref, out_ref):
    width, rows = q_ref.shape
    tile = rows // 2
    pos = pos_ref[0]
    has_left = pos >= 1
    has_far = pos >= 2
    j = lax.broadcasted_iota(jnp.int32, (tile, tile), 0)
    i = lax.broadcasted_iota(jnp.int32, (tile, tile), 1)
    after = j > i

    def head(h, carry):
        at = pl.ds(pl.multiple_of(h * HD, HD), HD)
        vt = pl.ds(pl.multiple_of(width + h * HD, HD), HD)
        for part in range(2):
            cols = slice(part * tile, (part + 1) * tile)
            q = q_ref[at, cols]
            pieces = [(far_ref, part * tile, (part + 1) * tile, has_far, 1)]
            if part == 0:
                pieces.append((far_ref, tile, rows, has_far, 0))
            pieces.append((left_ref, 0, rows, has_left, 0))
            if part == 1:
                pieces.append((own_ref, 0, tile, None, 0))
            pieces.append((own_ref, part * tile, (part + 1) * tile, None, 2))
            scores = []
            peak = None
            for ref, lo, hi, present, mask in pieces:
                s = tdot(ref[at, lo:hi], q)
                if mask == 1:
                    s = jnp.where(after, s, -FAR)
                elif mask == 2:
                    s = jnp.where(after, -FAR, s)
                top = jnp.max(s, axis=0, keepdims=True)
                if present is not None:
                    top = jnp.where(present, top, -FAR)
                peak = top if peak is None else jnp.maximum(peak, top)
                scores.append(s)
            peak = peak * LOG2E
            total = None
            acc = None
            for (ref, lo, hi, present, mask), s in zip(pieces, scores):
                less = peak if present is None else jnp.where(present, peak, FAR)
                p = jnp.exp2(s * LOG2E - less)
                add = jnp.sum(p, axis=0, keepdims=True)
                total = add if total is None else total + add
                o = jnp.dot(ref[vt, lo:hi], p.astype(jnp.bfloat16), preferred_element_type=jnp.float32)
                acc = o if acc is None else acc + o
            out_ref[at, cols] = (acc / total).astype(jnp.bfloat16)
        return carry

    lax.fori_loop(0, width // HD, head, 0)


def cross_body(pos_ref, q_ref, ends_ref, left_ref, own_ref, right_ref, out_ref):
    width, tokens = q_ref.shape
    rows = own_ref.shape[1]
    first = ends_ref[0:1, :]
    last = ends_ref[1:2, :]
    base = (pos_ref[0] - 1) * rows
    refs = (left_ref, own_ref, right_ref)
    keeps = []
    for n in range(3):
        kpos = lax.broadcasted_iota(jnp.int32, (rows, tokens), 0) + (base + n * rows)
        keeps.append((kpos >= first) & (kpos < last))

    for h in range(width // HD):
        at = slice(h * HD, (h + 1) * HD)
        vt = slice(width + h * HD, width + (h + 1) * HD)
        q = q_ref[at, :] * jnp.bfloat16(SCALE)
        scores = [jnp.where(keep, tdot(ref[at, :], q), -FAR) for ref, keep in zip(refs, keeps)]
        peak = functools.reduce(jnp.maximum, [jnp.max(s, axis=0, keepdims=True) for s in scores]) * LOG2E
        total = None
        acc = None
        for ref, s in zip(refs, scores):
            p = jnp.exp2(s * LOG2E - peak)
            add = jnp.sum(p, axis=0, keepdims=True)
            total = add if total is None else total + add
            o = jnp.dot(ref[vt, :], p.astype(jnp.bfloat16), preferred_element_type=jnp.float32)
            acc = o if acc is None else acc + o
        out_ref[at, :] = (acc / total).astype(jnp.bfloat16)


def out_body(dec_ref, own_ref, b1_ref, b2_ref, b3_ref, w_ref, resid_ref, out_ref, whole_ref):
    width = own_ref.shape[0]
    place(dec_ref[0], [(0, own_ref), (3, b1_ref), (2, b2_ref), (1, b3_ref)], whole_ref, width)
    mixed = jnp.dot(w_ref[...], whole_ref[...], preferred_element_type=jnp.float32)
    out_ref[...] = (resid_ref[...] + mixed).astype(jnp.bfloat16)


def local(frames, queries, align_start, align_end, gain_conv, conv_kernel, gain_attn, w_qkv, w_out):
    bf16, f32 = jnp.bfloat16, jnp.float32
    x = frames.T
    width, rows = x.shape
    tokens = queries.shape[0]
    dec = lax.axis_index("dec").astype(jnp.int32).reshape(1)
    pos = lax.axis_index("ctx").astype(jnp.int32).reshape(1)
    sds = jax.ShapeDtypeStruct

    b2, b1, b3 = rot(x, "dec", 2), rot(x, "dec", 1), rot(x, "dec", 3)
    from_left = shifted(frames[rows - RIM :], "ctx", 1)
    from_right = shifted(frames[:RIM], "ctx", -1)
    pay = call(
        pack_body,
        sds((72, width), f32),
        0,
        (from_left, from_right, conv_kernel, gain_conv[None], gain_attn[None]),
        mib=4,
        flops=50_000_000_000,
        nbytes=300_000,
    )
    pay = lax.all_gather(pay, "dec", axis=1, tiled=True)
    w_t = jnp.transpose(w_qkv, (1, 2, 0)).reshape(3 * width, D)
    w_t = call(hold_body, sds(w_t.shape, bf16), 0, (w_t,), hbm=1, mib=4, scratch=[pltpu.SemaphoreType.DMA], nbytes=5_000_000)
    wo_t = w_out.T
    ends = jnp.stack([jnp.repeat(align_start * FB, TB), jnp.repeat(align_end * FB, TB)], 0)
    ends = jnp.concatenate([ends, jnp.zeros((6, tokens), jnp.int32)], axis=0)

    q, kv, resid = call(
        front_body,
        (sds((width, rows), bf16), sds((2 * width, rows), bf16), sds((width, rows), f32)),
        1,
        (dec, x, b1, b2, b3, pay, w_t),
        mib=20,
        scratch=[
            pltpu.VMEM((D, rows), bf16),
            pltpu.VMEM((rows, LANES), f32),
            pltpu.VMEM((rows + 3 * RIM, LANES), f32),
            pltpu.VMEM((rows, LANES), f32),
            pltpu.VMEM((rows, LANES), f32),
            pltpu.VMEM((D // LANES, rows, LANES), f32),
            pltpu.VMEM((D, rows), f32),
            pltpu.VMEM((rows, D), bf16),
        ],
        flops=2 * 3 * width * D * rows,
        nbytes=5_000_000,
    )
    far = shifted(kv, "ctx", 2)
    left = shifted(kv, "ctx", 1)
    right = shifted(kv, "ctx", -1)
    attn = call(
        self_body,
        sds((width, rows), bf16),
        1,
        (pos, q, kv, left, far),
        flops=8 * width * rows * 1280,
        nbytes=2_500_000,
        exps=5 * rows * 1280,
    )
    a2, a1, a3 = rot(attn, "dec", 2), rot(attn, "dec", 1), rot(attn, "dec", 3)
    crossed = call(
        cross_body,
        sds((width, tokens), bf16),
        1,
        (pos, queries.T, ends, left, kv, right),
        flops=4 * width * tokens * 3 * rows,
        nbytes=2_000_000,
        exps=5 * tokens * 3 * rows,
    )
    encoded = call(
        out_body,
        sds((width, rows), bf16),
        1,
        (dec, attn, a1, a2, a3, wo_t, resid),
        scratch=[pltpu.VMEM((D, rows), bf16)],
        flops=2 * width * D * rows,
        nbytes=3_500_000,
    )
    return (encoded.T, crossed.T)


def solution(mesh):
    placed = (
        P("ctx", "dec"),
        P("ctx", "dec"),
        P("ctx"),
        P("ctx"),
        P("dec"),
        P(None, "dec"),
        P("dec"),
        P(None, None, "dec"),
        P(None, "dec"),
    )
    return jax.shard_map(
        local,
        mesh=mesh,
        in_specs=placed,
        out_specs=(P("ctx", "dec"), P("ctx", "dec")),
        check_vma=False,
    )
```

time: 180 us -> 118 us (0.66)
  the two profiles are of different devices: /device:TPU:128 before, /device:TPU:257 now
where the time goes in v1:
time: 118 us; the launch traced here: 117 us
  starting transfers between devices  36.8 us (31%)
  waiting for transfers between devices  27.7 us (23%)
  Pallas kernels  26.8 us (23%)
  blocking collectives  13.1 us (11%)
  local copies, waits for them, and re-layouts  11.7 us (10%)
    pallas_call x6, Pallas kernels, call(): pl.pallas_call(kernel, out_shape=outs, in_specs=specs, out_specs=jax.tree...  26.8 us
    ppermute x5, waiting for transfers between devices, shifted(): lax.ppermute(block, axis, [(i, i + distance) for i in devices if i + dist...  22.3 us
    ppermute x6, starting transfers between devices, rot(): lax.ppermute(block, axis, [(i, (i + distance) % count) for i in range(cou...  19.8 us
    ppermute x5, starting transfers between devices, shifted(): lax.ppermute(block, axis, [(i, i + distance) for i in devices if i + dist...  16.9 us
    all_gather x1, blocking collectives, local(): pay = lax.all_gather(pay, 'dec', axis=1, tiled=True)  13.1 us
    unnamed x25, local copies, waits for them, and re-layouts  8.01 us
    ppermute x6, waiting for transfers between devices, rot(): lax.ppermute(block, axis, [(i, (i + distance) % count) for i in range(cou...  5.41 us
  transfers between devices with their start and end apart: 11, of which 4 were waited for; matrix products, arithmetic and copies ran while one was open for 4% of the time, Pallas kernels for 11%

profile of v1, /device:TPU:257, one launch (start us, length us, event | category | flops | bytes accessed | tf_op | source)
XLA Modules:
  0.0 117.0 jit_solution(18366370218986206770)
XLA Ops:
  0.6 1.0 fusion
  1.7 3.7 %collective-permute-start.3 = (bf16[16,320]{1,0:T(8,128)(2,1)S(1)}, bf16[16,320]{1,0:T(8,128)(2,1)S(1)}, u32[]{:S(2)}, u32[]{:S(2)}) collective-permute-start(bf16[16,320]{1,0:T(8,128)(2,1)S(1)} %copy.17), channel_id=1, source_target_pairs={{0,4},{4,8},{8,12},{12,16},{16,20},{20,24},{24,28},{28,32},{32,36}... | collective-permute-start | bytes 30728 | tf_op jit(solution)/shard_map/ppermute | solution.py:49
  5.5 1.9 %collective-permute-start.4 = (bf16[16,320]{1,0:T(8,128)(2,1)S(1)}, bf16[16,320]{1,0:T(8,128)(2,1)S(1)}, u32[]{:S(2)}, u32[]{:S(2)}) collective-permute-start(bf16[16,320]{1,0:T(8,128)(2,1)S(1)} %copy.18), channel_id=1, source_target_pairs={{4,0},{8,4},{12,8},{16,12},{20,16},{24,20},{28,24},{32,28},{36,32}... | collective-permute-start | bytes 30728 | tf_op jit(solution)/shard_map/ppermute | solution.py:49
  7.4 3.2 %collective-permute-start = (bf16[320,512]{1,0:T(8,128)(2,1)}, bf16[320,512]{1,0:T(8,128)(2,1)S(1)}, u32[]{:S(2)}, u32[]{:S(2)}) collective-permute-start(bf16[320,512]{1,0:T(8,128)(2,1)} %bitcast.21), channel_id=1, source_target_pairs={{0,1},{1,2},{2,3},{3,0},{4,5},{5,6},{6,7},{7,4},{8,9},{9,10},{10,1... | collective-permute-start | bytes 983048 | tf_op jit(solution)/shard_map/ppermute | solution.py:44
  10.6 4.5 %collective-permute-start.1 = (bf16[320,512]{1,0:T(8,128)(2,1)}, bf16[320,512]{1,0:T(8,128)(2,1)}, u32[]{:S(2)}, u32[]{:S(2)}) collective-permute-start(bf16[320,512]{1,0:T(8,128)(2,1)} %bitcast.22), channel_id=1, source_target_pairs={{0,2},{1,3},{2,0},{3,1},{4,6},{5,7},{6,4},{7,5},{8,10},{9,11},{10,... | collective-permute-start | bytes 983048 | tf_op jit(solution)/shard_map/ppermute | solution.py:44
  15.2 3.0 %collective-permute-start.2 = (bf16[320,512]{1,0:T(8,128)(2,1)}, bf16[320,512]{1,0:T(8,128)(2,1)}, u32[]{:S(2)}, u32[]{:S(2)}) collective-permute-start(bf16[320,512]{1,0:T(8,128)(2,1)} %bitcast.23), channel_id=1, source_target_pairs={{0,3},{1,0},{2,1},{3,2},{4,7},{5,4},{6,5},{7,6},{8,11},{9,8},{10,9... | collective-permute-start | bytes 983048 | tf_op jit(solution)/shard_map/ppermute | solution.py:44
  18.2 0.7 broadcast_in_dim.15.gain1_ref
  18.9 0.7 broadcast_in_dim.16.gain2_ref
  19.5 1.7 %copy-done = bf16[1280,3,320]{0,2,1:T(8,128)(2,1)S(1)} copy-done((bf16[1280,3,320]{0,2,1:T(8,128)(2,1)S(1)}, bf16[1280,3,320]{0,2,1:T(8,128)(2,1)}, u32[]{:S(2)}) %copy-start) | copy-done | bytes 2457624
  21.6 0.5 copy-done.6
  22.1 13.1 %all-gather = f32[4,320,72]{1,2,0:T(8,128)S(1)} all-gather(f32[1,320,72]{1,2,0:T(8,128)S(1)} %bitcast.19), channel_id=1, replica_groups=mesh['ctx'=128,'dec'=4] {'dec'}, dimensions={0}, use_global_device_ids=true | all-gather | bytes 460800 | tf_op jit(solution)/shard_map/all_gather | solution.py:260
  35.2 0.9 copy.16
  36.0 1.3 %reshape.17 = f32[1280,72]{0,1:T(8,128)S(1)} reshape(f32[4,320,72]{1,0,2:T(4,128)} %copy.16) | data formatting | bytes 737280
  37.4 0.7 copy-done.4
  38.1 1.0 copy-done.3
  39.1 1.0 copy-done.5
  40.0 11.5 %shard_map.106 = (bf16[320,512]{1,0:T(8,128)(2,1)S(1)}, bf16[640,512]{1,0:T(8,128)(2,1)}, f32[320,512]{1,0:T(8,128)S(1)}) custom-call(s32[1]{0:T(128)} %bitcast.dec_ref, bf16[320,512]{1,0:T(8,128)(2,1)S(1)} %bitcast.24, bf16[320,512]{1,0:T(8,128)(2,1)S(1)} %copy-done.5, bf16[320,512]{1,0:T(8,128)(2,1)} %collective-permute-done.1.b2_ref, ...), custom_call_target="tpu_custom_call" | custom-call | flops 1258291200 | bytes 5000000 | tf_op jit(solution)/shard_map/pallas_call | solution.py:31
  51.5 0.7 copy-done.7
  52.3 6.6 %collective-permute-start.5 = (bf16[640,512]{1,0:T(8,128)(2,1)}, bf16[640,512]{1,0:T(8,128)(2,1)S(1)}, u32[]{:S(2)}, u32[]{:S(2)}) collective-permute-start(bf16[640,512]{1,0:T(8,128)(2,1)} %get-tuple-element.6.own_ref), channel_id=1, source_target_pairs={{0,4},{4,8},{8,12},{12,16},{16,20},{20,24},{24,28},{28,32},{32,36}... | collective-permute-start | bytes 1966088 | tf_op jit(solution)/shard_map/ppermute | solution.py:49
  58.9 2.8 %collective-permute-start.6 = (bf16[640,512]{1,0:T(8,128)(2,1)}, bf16[640,512]{1,0:T(8,128)(2,1)S(1)}, u32[]{:S(2)}, u32[]{:S(2)}) collective-permute-start(bf16[640,512]{1,0:T(8,128)(2,1)} %get-tuple-element.6.own_ref), channel_id=1, source_target_pairs={{0,8},{4,12},{8,16},{12,20},{16,24},{20,28},{24,32},{28,36},{32,40... | collective-permute-start | bytes 1966088 | tf_op jit(solution)/shard_map/ppermute | solution.py:49
  61.7 1.9 %collective-permute-start.10 = (bf16[640,512]{1,0:T(8,128)(2,1)}, bf16[640,512]{1,0:T(8,128)(2,1)S(1)}, u32[]{:S(2)}, u32[]{:S(2)}) collective-permute-start(bf16[640,512]{1,0:T(8,128)(2,1)} %get-tuple-element.6.own_ref), channel_id=1, source_target_pairs={{4,0},{8,4},{12,8},{16,12},{20,16},{24,20},{28,24},{32,28},{36,32}... | collective-permute-start | bytes 1966088 | tf_op jit(solution)/shard_map/ppermute | solution.py:49
  63.6 7.5 %collective-permute-done.5.left_ref = bf16[640,512]{1,0:T(8,128)(2,1)S(1)} collective-permute-done((bf16[640,512]{1,0:T(8,128)(2,1)}, bf16[640,512]{1,0:T(8,128)(2,1)S(1)}, u32[]{:S(2)}, u32[]{:S(2)}) %collective-permute-start.5) | collective-permute-done | bytes 655392 | tf_op jit(solution)/shard_map/ppermute | solution.py:49
  71.1 14.8 %collective-permute-done.6.far_ref = bf16[640,512]{1,0:T(8,128)(2,1)S(1)} collective-permute-done((bf16[640,512]{1,0:T(8,128)(2,1)}, bf16[640,512]{1,0:T(8,128)(2,1)S(1)}, u32[]{:S(2)}, u32[]{:S(2)}) %collective-permute-start.6) | collective-permute-done | bytes 655392 | tf_op jit(solution)/shard_map/ppermute | solution.py:49
  85.9 1.0 copy-done.8
  86.9 8.3 %shard_map.107.own_ref = bf16[320,512]{1,0:T(8,128)(2,1)S(1)} custom-call(s32[1]{0:T(128)} %bitcast.1.pos_ref, bf16[320,512]{1,0:T(8,128)(2,1)S(1)} %copy-done.8, bf16[640,512]{1,0:T(8,128)(2,1)} %get-tuple-element.6.own_ref, bf16[640,512]{1,0:T(8,128)(2,1)S(1)} %collective-permute-done.5.left_ref, bf16[640,512]{1,0:T(8,128)(2,1)S(1)} %collective-permute-done.6.far_ref), custom_call_target="tpu_custom_call" | custom-call | flops 1677721600 | bytes 2500000 | tf_op jit(solution)/shard_map/pallas_call | solution.py:31
  95.2 2.4 %collective-permute-start.7 = (bf16[320,512]{1,0:T(8,128)(2,1)S(1)}, bf16[320,512]{1,0:T(8,128)(2,1)S(1)}, u32[]{:S(2)}, u32[]{:S(2)}) collective-permute-start(bf16[320,512]{1,0:T(8,128)(2,1)S(1)} %shard_map.107.own_ref), channel_id=1, source_target_pairs={{0,1},{1,2},{2,3},{3,0},{4,5},{5,6},{6,7},{7,4},{8,9},{9,10},{10,1... | collective-permute-start | bytes 983048 | tf_op jit(solution)/shard_map/ppermute | solution.py:44
  97.6 4.3 %collective-permute-start.8 = (bf16[320,512]{1,0:T(8,128)(2,1)S(1)}, bf16[320,512]{1,0:T(8,128)(2,1)}, u32[]{:S(2)}, u32[]{:S(2)}) collective-permute-start(bf16[320,512]{1,0:T(8,128)(2,1)S(1)} %shard_map.107.own_ref), channel_id=1, source_target_pairs={{0,2},{1,3},{2,0},{3,1},{4,6},{5,7},{6,4},{7,5},{8,10},{9,11},{10,... | collective-permute-start | bytes 983048 | tf_op jit(solution)/shard_map/ppermute | solution.py:44
  101.9 2.4 %collective-permute-start.9 = (bf16[320,512]{1,0:T(8,128)(2,1)S(1)}, bf16[320,512]{1,0:T(8,128)(2,1)}, u32[]{:S(2)}, u32[]{:S(2)}) collective-permute-start(bf16[320,512]{1,0:T(8,128)(2,1)S(1)} %shard_map.107.own_ref), channel_id=1, source_target_pairs={{0,3},{1,0},{2,1},{3,2},{4,7},{5,4},{6,5},{7,6},{8,11},{9,8},{10,9... | collective-permute-start | bytes 983048 | tf_op jit(solution)/shard_map/ppermute | solution.py:44
  104.8 4.2 %shard_map.109 = bf16[320,128]{1,0:T(8,128)(2,1)} custom-call(s32[1]{0:T(128)} %bitcast.1.pos_ref, bf16[320,128]{1,0:T(8,128)(2,1)S(1)} %bitcast.20, s32[8,128]{1,0:T(8,128)S(1)} %add_add_fusion.ends_ref, bf16[640,512]{1,0:T(8,128)(2,1)S(1)} %collective-permute-done.5.left_ref, bf16[640,512]{1,0:T(8,128)(2,1)} %get-tuple-element.6.own_ref, ...), custom_call_target="tpu_custom_call" | custom-call | flops 251658240 | bytes 2000000 | tf_op jit(solution)/shard_map/pallas_call | solution.py:31
  109.1 2.7 %collective-permute-done.8.b2_ref = bf16[320,512]{1,0:T(8,128)(2,1)} collective-permute-done((bf16[320,512]{1,0:T(8,128)(2,1)S(1)}, bf16[320,512]{1,0:T(8,128)(2,1)}, u32[]{:S(2)}, u32[]{:S(2)}) %collective-permute-start.8) | collective-permute-done | bytes 327712 | tf_op jit(solution)/shard_map/ppermute | solution.py:44
  111.8 2.7 %collective-permute-done.9.b3_ref = bf16[320,512]{1,0:T(8,128)(2,1)} collective-permute-done((bf16[320,512]{1,0:T(8,128)(2,1)S(1)}, bf16[320,512]{1,0:T(8,128)(2,1)}, u32[]{:S(2)}, u32[]{:S(2)}) %collective-permute-start.9) | collective-permute-done | bytes 327712 | tf_op jit(solution)/shard_map/ppermute | solution.py:44
  114.5 2.5 %shard_map.108 = bf16[320,512]{1,0:T(8,128)(2,1)} custom-call(s32[1]{0:T(128)} %bitcast.dec_ref, bf16[320,512]{1,0:T(8,128)(2,1)S(1)} %shard_map.107.own_ref, bf16[320,512]{1,0:T(8,128)(2,1)S(1)} %collective-permute-done.7.b1_ref, bf16[320,512]{1,0:T(8,128)(2,1)} %collective-permute-done.8.b2_ref, bf16[320,512]{1,0:T(8,128)(2,1)} %collective-permute-done.9.b3_ref, ...), custom_call_target="tpu_custom_call" | custom-call | flops 419430400 | bytes 3500000 | tf_op jit(solution)/shard_map/pallas_call | solution.py:31
  (35 shorter events, 1.0 us)
Async XLA Ops:
  1.7 19.8 %collective-permute-start.3 = (bf16[16,320]{1,0:T(8,128)(2,1)S(1)}, bf16[16,320]{1,0:T(8,128)(2,1)S(1)}, u32[]{:S(2)}, u32[]{:S(2)}) collective-permute-start(bf16[16,320]{1,0:T(8,128)(2,1)S(1)} %copy.17), channel_id=1, source_target_pairs={{0,4},{4,8},{8,12},{12,16},{16,20},{20,24},{24,28},{28,32},{32,36}... | collective-permute-start | bytes 30728 | tf_op jit(solution)/shard_map/ppermute | solution.py:49
  5.5 16.1 %collective-permute-start.4 = (bf16[16,320]{1,0:T(8,128)(2,1)S(1)}, bf16[16,320]{1,0:T(8,128)(2,1)S(1)}, u32[]{:S(2)}, u32[]{:S(2)}) collective-permute-start(bf16[16,320]{1,0:T(8,128)(2,1)S(1)} %copy.18), channel_id=1, source_target_pairs={{4,0},{8,4},{12,8},{16,12},{20,16},{24,20},{28,24},{32,28},{36,32}... | collective-permute-start | bytes 30728 | tf_op jit(solution)/shard_map/ppermute | solution.py:49
  7.4 29.9 %collective-permute-start = (bf16[320,512]{1,0:T(8,128)(2,1)}, bf16[320,512]{1,0:T(8,128)(2,1)S(1)}, u32[]{:S(2)}, u32[]{:S(2)}) collective-permute-start(bf16[320,512]{1,0:T(8,128)(2,1)} %bitcast.21), channel_id=1, source_target_pairs={{0,1},{1,2},{2,3},{3,0},{4,5},{5,6},{6,7},{7,4},{8,9},{9,10},{10,1... | collective-permute-start | bytes 983048 | tf_op jit(solution)/shard_map/ppermute | solution.py:44
  10.6 27.5 %collective-permute-start.1 = (bf16[320,512]{1,0:T(8,128)(2,1)}, bf16[320,512]{1,0:T(8,128)(2,1)}, u32[]{:S(2)}, u32[]{:S(2)}) collective-permute-start(bf16[320,512]{1,0:T(8,128)(2,1)} %bitcast.22), channel_id=1, source_target_pairs={{0,2},{1,3},{2,0},{3,1},{4,6},{5,7},{6,4},{7,5},{8,10},{9,11},{10,... | collective-permute-start | bytes 983048 | tf_op jit(solution)/shard_map/ppermute | solution.py:44
  15.2 22.9 %collective-permute-start.2 = (bf16[320,512]{1,0:T(8,128)(2,1)}, bf16[320,512]{1,0:T(8,128)(2,1)}, u32[]{:S(2)}, u32[]{:S(2)}) collective-permute-start(bf16[320,512]{1,0:T(8,128)(2,1)} %bitcast.23), channel_id=1, source_target_pairs={{0,3},{1,0},{2,1},{3,2},{4,7},{5,4},{6,5},{7,6},{8,11},{9,8},{10,9... | collective-permute-start | bytes 983048 | tf_op jit(solution)/shard_map/ppermute | solution.py:44
  19.5 1.7 %copy-start = (bf16[1280,3,320]{0,2,1:T(8,128)(2,1)S(1)}, bf16[1280,3,320]{0,2,1:T(8,128)(2,1)}, u32[]{:S(2)}) copy-start(bf16[1280,3,320]{0,2,1:T(8,128)(2,1)} %param.16) | copy-start | bytes 7372804
  21.2 0.8 copy-start.6
  37.4 26.3 %copy-start.9 = (s32[4]{0:T(128)S(1)}, s32[4]{0:T(128)}, u32[]{:S(2)}) copy-start(s32[4]{0:T(128)} %param.11) | copy-start | bytes 52
  37.4 0.7 copy-start.4
  38.1 1.0 copy-start.3
  39.1 1.0 copy-start.5
  51.5 0.7 copy-start.7
  52.3 18.9 %collective-permute-start.5 = (bf16[640,512]{1,0:T(8,128)(2,1)}, bf16[640,512]{1,0:T(8,128)(2,1)S(1)}, u32[]{:S(2)}, u32[]{:S(2)}) collective-permute-start(bf16[640,512]{1,0:T(8,128)(2,1)} %get-tuple-element.6.own_ref), channel_id=1, source_target_pairs={{0,4},{4,8},{8,12},{12,16},{16,20},{20,24},{24,28},{28,32},{32,36}... | collective-permute-start | bytes 1966088 | tf_op jit(solution)/shard_map/ppermute | solution.py:49
  58.9 27.1 %collective-permute-start.6 = (bf16[640,512]{1,0:T(8,128)(2,1)}, bf16[640,512]{1,0:T(8,128)(2,1)S(1)}, u32[]{:S(2)}, u32[]{:S(2)}) collective-permute-start(bf16[640,512]{1,0:T(8,128)(2,1)} %get-tuple-element.6.own_ref), channel_id=1, source_target_pairs={{0,8},{4,12},{8,16},{12,20},{16,24},{20,28},{24,32},{28,36},{32,40... | collective-permute-start | bytes 1966088 | tf_op jit(solution)/shard_map/ppermute | solution.py:49
  61.7 43.2 %collective-permute-start.10 = (bf16[640,512]{1,0:T(8,128)(2,1)}, bf16[640,512]{1,0:T(8,128)(2,1)S(1)}, u32[]{:S(2)}, u32[]{:S(2)}) collective-permute-start(bf16[640,512]{1,0:T(8,128)(2,1)} %get-tuple-element.6.own_ref), channel_id=1, source_target_pairs={{4,0},{8,4},{12,8},{16,12},{20,16},{24,20},{28,24},{32,28},{36,32}... | collective-permute-start | bytes 1966088 | tf_op jit(solution)/shard_map/ppermute | solution.py:49
  85.9 1.0 copy-start.8
  86.9 17.5 %copy-start.10 = (s32[4]{0:T(128)S(1)}, s32[4]{0:T(128)}, u32[]{:S(2)}) copy-start(s32[4]{0:T(128)} %param.12) | copy-start | bytes 52
  86.9 18.0 %copy-start.2 = (bf16[128,320]{0,1:T(8,128)(2,1)S(1)}, bf16[128,320]{0,1:T(8,128)(2,1)}, u32[]{:S(2)}) copy-start(bf16[128,320]{0,1:T(8,128)(2,1)} %param.10) | copy-start | bytes 245764
  95.2 19.3 %copy-start.1 = (bf16[1280,320]{0,1:T(8,128)(2,1)S(1)}, bf16[1280,320]{0,1:T(8,128)(2,1)}, u32[]{:S(2)}) copy-start(bf16[1280,320]{0,1:T(8,128)(2,1)} %param.17) | copy-start | bytes 2457604
  95.2 13.9 %collective-permute-start.7 = (bf16[320,512]{1,0:T(8,128)(2,1)S(1)}, bf16[320,512]{1,0:T(8,128)(2,1)S(1)}, u32[]{:S(2)}, u32[]{:S(2)}) collective-permute-start(bf16[320,512]{1,0:T(8,128)(2,1)S(1)} %shard_map.107.own_ref), channel_id=1, source_target_pairs={{0,1},{1,2},{2,3},{3,0},{4,5},{5,6},{6,7},{7,4},{8,9},{9,10},{10,1... | collective-permute-start | bytes 983048 | tf_op jit(solution)/shard_map/ppermute | solution.py:44
  97.6 14.2 %collective-permute-start.8 = (bf16[320,512]{1,0:T(8,128)(2,1)S(1)}, bf16[320,512]{1,0:T(8,128)(2,1)}, u32[]{:S(2)}, u32[]{:S(2)}) collective-permute-start(bf16[320,512]{1,0:T(8,128)(2,1)S(1)} %shard_map.107.own_ref), channel_id=1, source_target_pairs={{0,2},{1,3},{2,0},{3,1},{4,6},{5,7},{6,4},{7,5},{8,10},{9,11},{10,... | collective-permute-start | bytes 983048 | tf_op jit(solution)/shard_map/ppermute | solution.py:44
  101.9 12.6 %collective-permute-start.9 = (bf16[320,512]{1,0:T(8,128)(2,1)S(1)}, bf16[320,512]{1,0:T(8,128)(2,1)}, u32[]{:S(2)}, u32[]{:S(2)}) collective-permute-start(bf16[320,512]{1,0:T(8,128)(2,1)S(1)} %shard_map.107.own_ref), channel_id=1, source_target_pairs={{0,3},{1,0},{2,1},{3,2},{4,7},{5,4},{6,5},{7,6},{8,11},{9,8},{10,9... | collective-permute-start | bytes 983048 | tf_op jit(solution)/shard_map/ppermute | solution.py:44

commit v2 on v1

--- a/solution.py
+++ b/solution.py
@@ -26,7 +26,7 @@
 HBM = pl.BlockSpec(memory_space=pltpu.HBM)
 
 
-def call(kernel, outs, smem, operands, scratch=(), hbm=0, mib=16, flops=0, nbytes=0, exps=0):
+def call(kernel, outs, smem, operands, scratch=(), hbm=0, mib=32, flops=0, nbytes=0, exps=0):
     specs = [SMEM] * smem + [VMEM] * (len(operands) - smem - hbm) + [HBM] * hbm
     return pl.pallas_call(
         kernel,
@@ -39,9 +39,13 @@
     )(*operands)
 
 
-def rot(block, axis, distance):
-    count = lax.axis_size(axis)
-    return lax.ppermute(block, axis, [(i, (i + distance) % count) for i in range(count)])
+def swapped(block, axis, bits):
+    return lax.ppermute(block, axis, [(i, i ^ bits) for i in range(lax.axis_size(axis))])
+
+
+def across(block, axis):
+    pairs = range(1, lax.axis_size(axis) - 1, 2)
+    return lax.ppermute(block, axis, [(i, i + 1) for i in pairs] + [(i + 1, i) for i in pairs])
 
 
 def shifted(block, axis, distance):
@@ -49,24 +53,20 @@
     return lax.ppermute(block, axis, [(i, i + distance) for i in devices if i + distance in devices])
 
 
-def pack_body(left_ref, right_ref, taps_ref, gain1_ref, gain2_ref, out_ref):
-    out_ref[0:RIM, :] = left_ref[...].astype(jnp.float32)
-    out_ref[RIM : 2 * RIM, :] = right_ref[...].astype(jnp.float32)
+def pack_body(pos_ref, near_ref, other_ref, taps_ref, gains_ref, out_ref):
+    odd = lax.rem(pos_ref[0], 2) == 1
+    near = near_ref[...].astype(jnp.float32)
+    other = other_ref[...].astype(jnp.float32)
+    out_ref[0:RIM, :] = jnp.where(odd, near, other)
+    out_ref[RIM : 2 * RIM, :] = jnp.where(odd, other, near)
     out_ref[2 * RIM : 2 * RIM + KW, :] = taps_ref[...]
-    out_ref[2 * RIM + KW : 2 * RIM + KW + 1, :] = gain1_ref[...]
-    out_ref[2 * RIM + KW + 1 : 2 * RIM + KW + 2, :] = gain2_ref[...]
+    out_ref[2 * RIM + KW : 2 * RIM + KW + 2, :] = gains_ref[...]
     out_ref[2 * RIM + KW + 2 :, :] = jnp.zeros((7, out_ref.shape[1]), jnp.float32)
-
-
-def hold_body(in_ref, out_ref, sem):
-    copy = pltpu.make_async_copy(in_ref, out_ref, sem)
-    copy.start()
-    copy.wait()
 
 
 def place(dec, blocks, whole_ref, width):
     for offset, block in blocks:
-        at = pl.multiple_of(lax.rem(dec + offset, 4) * width, width)
+        at = pl.multiple_of((dec ^ offset) * width, width)
         whole_ref[pl.ds(at, width), :] = block[:width, :]
 
 
@@ -75,12 +75,16 @@
 
 
 def front_body(
-    dec_ref, own_ref, b1_ref, b2_ref, b3_ref, pay_ref, w_ref, q_ref, kv_ref, resid_ref,
-    xall_ref, x_ref, pad_ref, scale_ref, square_ref, whole_ref, turned_ref, norm_ref,
+    dec_ref, own_ref, b1_ref, b2_ref, b3_ref, pays_ref, w_hbm, q_ref, kv_ref, resid_ref,
+    xall_ref, x_ref, pad_ref, scale_ref, square_ref, whole_ref, turned_ref, norm_ref, pay_ref, w_ref, sem,
 ):
     width, rows = own_ref.shape
     dec = dec_ref[0]
-    place(dec, [(0, own_ref), (3, b1_ref), (2, b2_ref), (1, b3_ref)], xall_ref, width)
+    fetch = pltpu.make_async_copy(w_hbm, w_ref, sem)
+    fetch.start()
+    place(dec, [(0, own_ref), (1, b1_ref), (2, b2_ref), (3, b3_ref)], xall_ref, width)
+    for n in range(4):
+        pay_ref[:, n * width : (n + 1) * width] = pays_ref[n]
     tiles = D // LANES
 
     def gather_square(f, total):
@@ -131,6 +135,7 @@
         lanes = slice(f * LANES, (f + 1) * LANES)
         gain = pay_ref[2 * RIM + KW + 1 : 2 * RIM + KW + 2, lanes]
         norm_ref[:, lanes] = (whole_ref[f] * scale2 * gain).astype(jnp.bfloat16)
+    fetch.wait()
     for third in (1, 2, 0):
         proj = lax.dot_general(
             w_ref[third * width : (third + 1) * width, :],
@@ -148,10 +153,11 @@
     return lax.dot_general(left, right, (((0,), (0,)), ((), ())), preferred_element_type=jnp.float32)
 
 
-def self_body(pos_ref, q_ref, own_ref, left_ref, far_ref, out_ref):
+def self_body(pos_ref, q_ref, own_ref, beside_ref, beyond_ref, far_ref, out_ref, left_ref):
     width, rows = q_ref.shape
     tile = rows // 2
     pos = pos_ref[0]
+    left_ref[...] = jnp.where(lax.rem(pos, 2) == 1, beside_ref[...], beyond_ref[...])
     has_left = pos >= 1
     has_far = pos >= 2
     j = lax.broadcasted_iota(jnp.int32, (tile, tile), 0)
@@ -200,16 +206,17 @@
     lax.fori_loop(0, width // HD, head, 0)
 
 
-def cross_body(pos_ref, q_ref, ends_ref, left_ref, own_ref, right_ref, out_ref):
+def cross_body(pos_ref, q_ref, ends_ref, beside_ref, own_ref, beyond_ref, out_ref):
     width, tokens = q_ref.shape
     rows = own_ref.shape[1]
     first = ends_ref[0:1, :]
     last = ends_ref[1:2, :]
-    base = (pos_ref[0] - 1) * rows
-    refs = (left_ref, own_ref, right_ref)
+    pos = pos_ref[0]
+    refs = (beside_ref, own_ref, beyond_ref)
+    places = (pos ^ 1, pos, jnp.where(lax.rem(pos, 2) == 1, pos + 1, pos - 1))
     keeps = []
     for n in range(3):
-        kpos = lax.broadcasted_iota(jnp.int32, (rows, tokens), 0) + (base + n * rows)
+        kpos = lax.broadcasted_iota(jnp.int32, (rows, tokens), 0) + places[n] * rows
         keeps.append((kpos >= first) & (kpos < last))
 
     for h in range(width // HD):
@@ -231,7 +238,7 @@
 
 def out_body(dec_ref, own_ref, b1_ref, b2_ref, b3_ref, w_ref, resid_ref, out_ref, whole_ref):
     width = own_ref.shape[0]
-    place(dec_ref[0], [(0, own_ref), (3, b1_ref), (2, b2_ref), (1, b3_ref)], whole_ref, width)
+    place(dec_ref[0], [(0, own_ref), (1, b1_ref), (2, b2_ref), (3, b3_ref)], whole_ref, width)
     mixed = jnp.dot(w_ref[...], whole_ref[...], preferred_element_type=jnp.float32)
     out_ref[...] = (resid_ref[...] + mixed).astype(jnp.bfloat16)
 
@@ -245,21 +252,21 @@
     pos = lax.axis_index("ctx").astype(jnp.int32).reshape(1)
     sds = jax.ShapeDtypeStruct
 
-    b2, b1, b3 = rot(x, "dec", 2), rot(x, "dec", 1), rot(x, "dec", 3)
-    from_left = shifted(frames[rows - RIM :], "ctx", 1)
-    from_right = shifted(frames[:RIM], "ctx", -1)
+    head, tail = frames[:RIM], frames[rows - RIM :]
+    odd = lax.rem(pos[0], 2) == 1
+    near = swapped(jnp.where(odd, head, tail), "ctx", 1)
+    other = across(jnp.where(odd, tail, head), "ctx")
+    b2, b1, b3 = swapped(x, "dec", 2), swapped(x, "dec", 1), swapped(x, "dec", 3)
     pay = call(
         pack_body,
         sds((72, width), f32),
-        0,
-        (from_left, from_right, conv_kernel, gain_conv[None], gain_attn[None]),
-        mib=4,
+        1,
+        (pos, near, other, conv_kernel, jnp.stack([gain_conv, gain_attn])),
         flops=50_000_000_000,
         nbytes=300_000,
     )
-    pay = lax.all_gather(pay, "dec", axis=1, tiled=True)
+    pay = lax.all_gather(pay, "dec", axis=0)
     w_t = jnp.transpose(w_qkv, (1, 2, 0)).reshape(3 * width, D)
-    w_t = call(hold_body, sds(w_t.shape, bf16), 0, (w_t,), hbm=1, mib=4, scratch=[pltpu.SemaphoreType.DMA], nbytes=5_000_000)
     wo_t = w_out.T
     ends = jnp.stack([jnp.repeat(align_start * FB, TB), jnp.repeat(align_end * FB, TB)], 0)
     ends = jnp.concatenate([ends, jnp.zeros((6, tokens), jnp.int32)], axis=0)
@@ -269,7 +276,8 @@
         (sds((width, rows), bf16), sds((2 * width, rows), bf16), sds((width, rows), f32)),
         1,
         (dec, x, b1, b2, b3, pay, w_t),
-        mib=20,
+        hbm=1,
+        mib=48,
         scratch=[
             pltpu.VMEM((D, rows), bf16),
             pltpu.VMEM((rows, LANES), f32),
@@ -279,28 +287,32 @@
             pltpu.VMEM((D // LANES, rows, LANES), f32),
             pltpu.VMEM((D, rows), f32),
             pltpu.VMEM((rows, D), bf16),
+            pltpu.VMEM((72, D), f32),
+            pltpu.VMEM((3 * width, D), bf16),
+            pltpu.SemaphoreType.DMA,
         ],
         flops=2 * 3 * width * D * rows,
         nbytes=5_000_000,
     )
     far = shifted(kv, "ctx", 2)
-    left = shifted(kv, "ctx", 1)
-    right = shifted(kv, "ctx", -1)
+    beyond = across(kv, "ctx")
+    beside = swapped(kv, "ctx", 1)
     attn = call(
         self_body,
         sds((width, rows), bf16),
         1,
-        (pos, q, kv, left, far),
+        (pos, q, kv, beside, beyond, far),
+        scratch=[pltpu.VMEM((2 * width, rows), bf16)],
         flops=8 * width * rows * 1280,
         nbytes=2_500_000,
         exps=5 * rows * 1280,
     )
-    a2, a1, a3 = rot(attn, "dec", 2), rot(attn, "dec", 1), rot(attn, "dec", 3)
+    a2, a1, a3 = swapped(attn, "dec", 2), swapped(attn, "dec", 1), swapped(attn, "dec", 3)
     crossed = call(
         cross_body,
         sds((width, tokens), bf16),
         1,
-        (pos, queries.T, ends, left, kv, right),
+        (pos, queries.T, ends, beside, kv, beyond),
         flops=4 * width * tokens * 3 * rows,
         nbytes=2_000_000,
         exps=5 * tokens * 3 * rows,

time: 118 us -> 101 us (0.86)
  the two profiles are of different devices: /device:TPU:257 before, /device:TPU:100 now
where the time goes in v2:
time: 101 us
  starting transfers between devices  37.3 us (37%)
  Pallas kernels  24.4 us (24%)
  waiting for transfers between devices  20.9 us (21%)
  blocking collectives  13.3 us (13%)
  local copies, waits for them, and re-layouts  3.76 us (4%)
    ppermute x8, starting transfers between devices, swapped(): lax.ppermute(block, axis, [(i, i ^ bits) for i in range(lax.axis_size(axi...  28.6 us
    pallas_call x5, Pallas kernels, call(): pl.pallas_call(kernel, out_shape=outs, in_specs=specs, out_specs=jax.tree...  24.4 us
    all_gather x1, blocking collectives, local(): pay = lax.all_gather(pay, 'dec', axis=0)  13.3 us
    ppermute x8, waiting for transfers between devices, swapped(): lax.ppermute(block, axis, [(i, i ^ bits) for i in range(lax.axis_size(axi...  9.84 us
    ppermute x1, waiting for transfers between devices, shifted(): lax.ppermute(block, axis, [(i, i + distance) for i in devices if i + dist...  7.64 us
    ppermute x1, starting transfers between devices, shifted(): lax.ppermute(block, axis, [(i, i + distance) for i in devices if i + dist...  4.95 us
    ppermute x2, starting transfers between devices, across(): lax.ppermute(block, axis, [(i, i + 1) for i in pairs] + [(i + 1, i) for i...  3.84 us
    ppermute x2, waiting for transfers between devices, across(): lax.ppermute(block, axis, [(i, i + 1) for i in pairs] + [(i + 1, i) for i...  3.44 us
  transfers between devices with their start and end apart: 11, of which 4 were waited for; matrix products, arithmetic and copies ran while one was open for 3% of the time, Pallas kernels for 3%

profile of v2, /device:TPU:100, one launch (start us, length us, event | category | flops | bytes accessed | tf_op | source)
XLA Modules:
  0.0 100.7 jit_solution(16663292435668388807)
XLA Ops:
  0.6 4.9 %collective-permute-start.2 = (bf16[320,512]{1,0:T(8,128)(2,1)}, bf16[320,512]{1,0:T(8,128)(2,1)S(1)}, u32[]{:S(2)}, u32[]{:S(2)}) collective-permute-start(bf16[320,512]{1,0:T(8,128)(2,1)} %bitcast.14), channel_id=1, source_target_pairs={{0,3},{1,2},{2,1},{3,0},{4,7},{5,6},{6,5},{7,4},{8,11},{9,10},{10,... | collective-permute-start | bytes 983048 | tf_op jit(solution)/shard_map/ppermute | solution.py:43
  5.6 2.5 %collective-permute-start.1 = (bf16[320,512]{1,0:T(8,128)(2,1)}, bf16[320,512]{1,0:T(8,128)(2,1)S(1)}, u32[]{:S(2)}, u32[]{:S(2)}) collective-permute-start(bf16[320,512]{1,0:T(8,128)(2,1)} %bitcast.15), channel_id=1, source_target_pairs={{0,2},{1,3},{2,0},{3,1},{4,6},{5,7},{6,4},{7,5},{8,10},{9,11},{10,... | collective-permute-start | bytes 983048 | tf_op jit(solution)/shard_map/ppermute | solution.py:43
  8.1 2.4 %collective-permute-start = (bf16[320,512]{1,0:T(8,128)(2,1)}, bf16[320,512]{1,0:T(8,128)(2,1)S(1)}, u32[]{:S(2)}, u32[]{:S(2)}) collective-permute-start(bf16[320,512]{1,0:T(8,128)(2,1)} %bitcast.16), channel_id=1, source_target_pairs={{0,1},{1,0},{2,3},{3,2},{4,5},{5,4},{6,7},{7,6},{8,9},{9,8},{10,11... | collective-permute-start | bytes 983048 | tf_op jit(solution)/shard_map/ppermute | solution.py:43
  10.5 1.0 %fusion = (bf16[16,320]{0,1:T(8,128)(2,1)S(1)}, bf16[16,320]{0,1:T(8,128)(2,1)S(1)}) fusion(bf16[512,320]{0,1:T(8,128)(2,1)} %param.9), kind=kLoop, calls=%fused_computation.6 | loop fusion | bytes 40960 | tf_op jit(solution)/shard_map/slice | solution.py:255
  11.5 0.1 copy.14
  11.6 0.1 copy.13
  11.7 1.9 %collective-permute-start.4 = (bf16[16,320]{1,0:T(8,128)(2,1)S(1)}, bf16[16,320]{1,0:T(8,128)(2,1)S(1)}, u32[]{:S(2)}, u32[]{:S(2)}) collective-permute-start(bf16[16,320]{1,0:T(8,128)(2,1)S(1)} %get-tuple-element.10), channel_id=1, source_target_pairs={{4,8},{12,16},{20,24},{28,32},{36,40},{44,48},{52,56},{60,64},{68,... | collective-permute-start | bytes 30728 | tf_op jit(solution)/shard_map/ppermute | solution.py:48
  13.6 3.2 %collective-permute-start.3 = (bf16[16,320]{1,0:T(8,128)(2,1)S(1)}, bf16[16,320]{1,0:T(8,128)(2,1)S(1)}, u32[]{:S(2)}, u32[]{:S(2)}) collective-permute-start(bf16[16,320]{1,0:T(8,128)(2,1)S(1)} %get-tuple-element.11), channel_id=1, source_target_pairs={{0,4},{4,0},{8,12},{12,8},{16,20},{20,16},{24,28},{28,24},{32,36},... | collective-permute-start | bytes 30728 | tf_op jit(solution)/shard_map/ppermute | solution.py:43
  16.8 0.7 stack.9
  17.5 0.7 stack.10
  18.3 0.8 copy-done.4
  19.1 13.3 %all-gather = f32[288,320]{1,0:T(8,128)S(1)} all-gather(f32[72,320]{1,0:T(8,128)S(1)} %shard_map.104), channel_id=2, replica_groups=mesh['ctx'=128,'dec'=4] {'dec'}, dimensions={0}, use_global_device_ids=true | all-gather | bytes 460800 | tf_op jit(solution)/shard_map/all_gather | solution.py:268
  32.4 10.6 %shard_map.105 = (bf16[320,512]{1,0:T(8,128)(2,1)S(1)}, bf16[640,512]{1,0:T(8,128)(2,1)S(1)}, f32[320,512]{1,0:T(8,128)S(1)}) custom-call(s32[1]{0:T(128)} %bitcast.dec_ref, bf16[320,512]{1,0:T(8,128)(2,1)S(1)} %bitcast.17, bf16[320,512]{1,0:T(8,128)(2,1)S(1)} %collective-permute-done.b1_ref, bf16[320,512]{1,0:T(8,128)(2,1)S(1)} %collective-permute-done.1.b2_ref, ...), custom_call_target="tpu_custom_call" | custom-call | flops 1258291200 | bytes 5000000 | tf_op jit(solution)/shard_map/pallas_call | solution.py:31
  43.0 5.0 %collective-permute-start.7 = (bf16[640,512]{1,0:T(8,128)(2,1)S(1)}, bf16[640,512]{1,0:T(8,128)(2,1)S(1)}, u32[]{:S(2)}, u32[]{:S(2)}) collective-permute-start(bf16[640,512]{1,0:T(8,128)(2,1)S(1)} %get-tuple-element.6.own_ref), channel_id=1, source_target_pairs={{0,8},{4,12},{8,16},{12,20},{16,24},{20,28},{24,32},{28,36},{32,40... | collective-permute-start | bytes 1966088 | tf_op jit(solution)/shard_map/ppermute | solution.py:53
  48.0 1.9 %collective-permute-start.6 = (bf16[640,512]{1,0:T(8,128)(2,1)S(1)}, bf16[640,512]{1,0:T(8,128)(2,1)S(1)}, u32[]{:S(2)}, u32[]{:S(2)}) collective-permute-start(bf16[640,512]{1,0:T(8,128)(2,1)S(1)} %get-tuple-element.6.own_ref), channel_id=1, source_target_pairs={{4,8},{12,16},{20,24},{28,32},{36,40},{44,48},{52,56},{60,64},{68,... | collective-permute-start | bytes 1966088 | tf_op jit(solution)/shard_map/ppermute | solution.py:48
  49.9 5.6 %collective-permute-start.5 = (bf16[640,512]{1,0:T(8,128)(2,1)S(1)}, bf16[640,512]{1,0:T(8,128)(2,1)S(1)}, u32[]{:S(2)}, u32[]{:S(2)}) collective-permute-start(bf16[640,512]{1,0:T(8,128)(2,1)S(1)} %get-tuple-element.6.own_ref), channel_id=1, source_target_pairs={{0,4},{4,0},{8,12},{12,8},{16,20},{20,16},{24,28},{28,24},{32,36},... | collective-permute-start | bytes 1966088 | tf_op jit(solution)/shard_map/ppermute | solution.py:43
  55.5 7.6 %collective-permute-done.7.far_ref = bf16[640,512]{1,0:T(8,128)(2,1)S(1)} collective-permute-done((bf16[640,512]{1,0:T(8,128)(2,1)S(1)}, bf16[640,512]{1,0:T(8,128)(2,1)S(1)}, u32[]{:S(2)}, u32[]{:S(2)}) %collective-permute-start.7) | collective-permute-done | bytes 655392 | tf_op jit(solution)/shard_map/ppermute | solution.py:53
  63.1 3.4 %collective-permute-done.6.beyond_ref = bf16[640,512]{1,0:T(8,128)(2,1)S(1)} collective-permute-done((bf16[640,512]{1,0:T(8,128)(2,1)S(1)}, bf16[640,512]{1,0:T(8,128)(2,1)S(1)}, u32[]{:S(2)}, u32[]{:S(2)}) %collective-permute-start.6) | collective-permute-done | bytes 655392 | tf_op jit(solution)/shard_map/ppermute | solution.py:48
  66.6 8.0 %shard_map.106.own_ref = bf16[320,512]{1,0:T(8,128)(2,1)} custom-call(s32[1]{0:T(128)} %bitcast.1.pos_ref, bf16[320,512]{1,0:T(8,128)(2,1)S(1)} %get-tuple-element.5.q_ref, bf16[640,512]{1,0:T(8,128)(2,1)S(1)} %get-tuple-element.6.own_ref, bf16[640,512]{1,0:T(8,128)(2,1)S(1)} %collective-permute-done.5.beside_ref, ...), custom_call_target="tpu_custom_call" | custom-call | flops 1677721600 | bytes 2500000 | tf_op jit(solution)/shard_map/pallas_call | solution.py:31
  74.6 3.6 %collective-permute-start.10 = (bf16[320,512]{1,0:T(8,128)(2,1)}, bf16[320,512]{1,0:T(8,128)(2,1)}, u32[]{:S(2)}, u32[]{:S(2)}) collective-permute-start(bf16[320,512]{1,0:T(8,128)(2,1)} %shard_map.106.own_ref), channel_id=1, source_target_pairs={{0,3},{1,2},{2,1},{3,0},{4,7},{5,6},{6,5},{7,4},{8,11},{9,10},{10,... | collective-permute-start | bytes 983048 | tf_op jit(solution)/shard_map/ppermute | solution.py:43
  78.2 2.8 %collective-permute-start.9 = (bf16[320,512]{1,0:T(8,128)(2,1)}, bf16[320,512]{1,0:T(8,128)(2,1)}, u32[]{:S(2)}, u32[]{:S(2)}) collective-permute-start(bf16[320,512]{1,0:T(8,128)(2,1)} %shard_map.106.own_ref), channel_id=1, source_target_pairs={{0,2},{1,3},{2,0},{3,1},{4,6},{5,7},{6,4},{7,5},{8,10},{9,11},{10,... | collective-permute-start | bytes 983048 | tf_op jit(solution)/shard_map/ppermute | solution.py:43
  81.0 3.5 %collective-permute-start.8 = (bf16[320,512]{1,0:T(8,128)(2,1)}, bf16[320,512]{1,0:T(8,128)(2,1)}, u32[]{:S(2)}, u32[]{:S(2)}) collective-permute-start(bf16[320,512]{1,0:T(8,128)(2,1)} %shard_map.106.own_ref), channel_id=1, source_target_pairs={{0,1},{1,0},{2,3},{3,2},{4,5},{5,4},{6,7},{7,6},{8,9},{9,8},{10,11... | collective-permute-start | bytes 983048 | tf_op jit(solution)/shard_map/ppermute | solution.py:43
  84.6 0.1 pad.2.clone
  84.7 0.1 broadcast_in_dim.10
  84.7 0.1 stack_reshape.7
  84.8 0.1 broadcast_in_dim.9
  84.9 0.1 stack_reshape.6
  85.0 0.1 add_add_fusion.ends_ref
  85.0 3.1 %shard_map.108 = bf16[320,128]{1,0:T(8,128)(2,1)} custom-call(s32[1]{0:T(128)} %bitcast.1.pos_ref, bf16[320,128]{1,0:T(8,128)(2,1)S(1)} %bitcast.13, s32[8,128]{1,0:T(8,128)S(1)} %add_add_fusion.ends_ref, bf16[640,512]{1,0:T(8,128)(2,1)S(1)} %collective-permute-done.5.beside_ref, bf16[640,512]{1,0:T(8,128)(2,1)S(1)} %get-tuple-element.6.own_ref, ...), custom_call_target="tpu_custom_call" | custom-call | flops 251658240 | bytes 2000000 | tf_op jit(solution)/shard_map/pallas_call | solution.py:31
  88.2 7.3 %collective-permute-done.10.b3_ref = bf16[320,512]{1,0:T(8,128)(2,1)} collective-permute-done((bf16[320,512]{1,0:T(8,128)(2,1)}, bf16[320,512]{1,0:T(8,128)(2,1)}, u32[]{:S(2)}, u32[]{:S(2)}) %collective-permute-start.10) | collective-permute-done | bytes 327712 | tf_op jit(solution)/shard_map/ppermute | solution.py:43
  95.4 2.6 %collective-permute-done.8.b1_ref = bf16[320,512]{1,0:T(8,128)(2,1)} collective-permute-done((bf16[320,512]{1,0:T(8,128)(2,1)}, bf16[320,512]{1,0:T(8,128)(2,1)}, u32[]{:S(2)}, u32[]{:S(2)}) %collective-permute-start.8) | collective-permute-done | bytes 327712 | tf_op jit(solution)/shard_map/ppermute | solution.py:43
  98.0 2.7 %shard_map.107 = bf16[320,512]{1,0:T(8,128)(2,1)} custom-call(s32[1]{0:T(128)} %bitcast.dec_ref, bf16[320,512]{1,0:T(8,128)(2,1)} %shard_map.106.own_ref, bf16[320,512]{1,0:T(8,128)(2,1)} %collective-permute-done.8.b1_ref, bf16[320,512]{1,0:T(8,128)(2,1)} %collective-permute-done.9.b2_ref, bf16[320,512]{1,0:T(8,128)(2,1)} %collective-permute-done.10.b3_ref, ...), custom_call_target="tpu_custom_call" | custom-call | flops 419430400 | bytes 3500000 | tf_op jit(solution)/shard_map/pallas_call | solution.py:31
  (26 shorter events, 0.1 us)
Async XLA Ops:
  0.6 31.7 %collective-permute-start.2 = (bf16[320,512]{1,0:T(8,128)(2,1)}, bf16[320,512]{1,0:T(8,128)(2,1)S(1)}, u32[]{:S(2)}, u32[]{:S(2)}) collective-permute-start(bf16[320,512]{1,0:T(8,128)(2,1)} %bitcast.14), channel_id=1, source_target_pairs={{0,3},{1,2},{2,1},{3,0},{4,7},{5,6},{6,5},{7,4},{8,11},{9,10},{10,... | collective-permute-start | bytes 983048 | tf_op jit(solution)/shard_map/ppermute | solution.py:43
  5.6 26.8 %collective-permute-start.1 = (bf16[320,512]{1,0:T(8,128)(2,1)}, bf16[320,512]{1,0:T(8,128)(2,1)S(1)}, u32[]{:S(2)}, u32[]{:S(2)}) collective-permute-start(bf16[320,512]{1,0:T(8,128)(2,1)} %bitcast.15), channel_id=1, source_target_pairs={{0,2},{1,3},{2,0},{3,1},{4,6},{5,7},{6,4},{7,5},{8,10},{9,11},{10,... | collective-permute-start | bytes 983048 | tf_op jit(solution)/shard_map/ppermute | solution.py:43
  8.1 24.3 %collective-permute-start = (bf16[320,512]{1,0:T(8,128)(2,1)}, bf16[320,512]{1,0:T(8,128)(2,1)S(1)}, u32[]{:S(2)}, u32[]{:S(2)}) collective-permute-start(bf16[320,512]{1,0:T(8,128)(2,1)} %bitcast.16), channel_id=1, source_target_pairs={{0,1},{1,0},{2,3},{3,2},{4,5},{5,4},{6,7},{7,6},{8,9},{9,8},{10,11... | collective-permute-start | bytes 983048 | tf_op jit(solution)/shard_map/ppermute | solution.py:43
  11.7 6.5 %collective-permute-start.4 = (bf16[16,320]{1,0:T(8,128)(2,1)S(1)}, bf16[16,320]{1,0:T(8,128)(2,1)S(1)}, u32[]{:S(2)}, u32[]{:S(2)}) collective-permute-start(bf16[16,320]{1,0:T(8,128)(2,1)S(1)} %get-tuple-element.10), channel_id=1, source_target_pairs={{4,8},{12,16},{20,24},{28,32},{36,40},{44,48},{52,56},{60,64},{68,... | collective-permute-start | bytes 30728 | tf_op jit(solution)/shard_map/ppermute | solution.py:48
  13.6 4.6 %collective-permute-start.3 = (bf16[16,320]{1,0:T(8,128)(2,1)S(1)}, bf16[16,320]{1,0:T(8,128)(2,1)S(1)}, u32[]{:S(2)}, u32[]{:S(2)}) collective-permute-start(bf16[16,320]{1,0:T(8,128)(2,1)S(1)} %get-tuple-element.11), channel_id=1, source_target_pairs={{0,4},{4,0},{8,12},{12,8},{16,20},{20,16},{24,28},{28,24},{32,36},... | collective-permute-start | bytes 30728 | tf_op jit(solution)/shard_map/ppermute | solution.py:43
  18.3 0.8 copy-start.4
  19.1 13.3 %copy-start.2 = (bf16[512,320]{0,1:T(8,128)(2,1)S(1)}, bf16[512,320]{0,1:T(8,128)(2,1)}, u32[]{:S(2)}) copy-start(bf16[512,320]{0,1:T(8,128)(2,1)} %param.9) | copy-start | bytes 983044
  19.1 13.3 %copy-start.3 = (bf16[1280,3,320]{0,2,1:T(8,128)(2,1)S(1)}, bf16[1280,3,320]{0,2,1:T(8,128)(2,1)}, u32[]{:S(2)}) copy-start(bf16[1280,3,320]{0,2,1:T(8,128)(2,1)} %param.16) | copy-start | bytes 7372804
  32.3 23.1 %copy-start.5 = (s32[4]{0:T(128)S(1)}, s32[4]{0:T(128)}, u32[]{:S(2)}) copy-start(s32[4]{0:T(128)} %param.11) | copy-start | bytes 52
  43.0 20.1 %collective-permute-start.7 = (bf16[640,512]{1,0:T(8,128)(2,1)S(1)}, bf16[640,512]{1,0:T(8,128)(2,1)S(1)}, u32[]{:S(2)}, u32[]{:S(2)}) collective-permute-start(bf16[640,512]{1,0:T(8,128)(2,1)S(1)} %get-tuple-element.6.own_ref), channel_id=1, source_target_pairs={{0,8},{4,12},{8,16},{12,20},{16,24},{20,28},{24,32},{28,36},{32,40... | collective-permute-start | bytes 1966088 | tf_op jit(solution)/shard_map/ppermute | solution.py:53
  48.0 18.6 %collective-permute-start.6 = (bf16[640,512]{1,0:T(8,128)(2,1)S(1)}, bf16[640,512]{1,0:T(8,128)(2,1)S(1)}, u32[]{:S(2)}, u32[]{:S(2)}) collective-permute-start(bf16[640,512]{1,0:T(8,128)(2,1)S(1)} %get-tuple-element.6.own_ref), channel_id=1, source_target_pairs={{4,8},{12,16},{20,24},{28,32},{36,40},{44,48},{52,56},{60,64},{68,... | collective-permute-start | bytes 1966088 | tf_op jit(solution)/shard_map/ppermute | solution.py:48
  49.9 16.7 %collective-permute-start.5 = (bf16[640,512]{1,0:T(8,128)(2,1)S(1)}, bf16[640,512]{1,0:T(8,128)(2,1)S(1)}, u32[]{:S(2)}, u32[]{:S(2)}) collective-permute-start(bf16[640,512]{1,0:T(8,128)(2,1)S(1)} %get-tuple-element.6.own_ref), channel_id=1, source_target_pairs={{0,4},{4,0},{8,12},{12,8},{16,20},{20,16},{24,28},{28,24},{32,36},... | collective-permute-start | bytes 1966088 | tf_op jit(solution)/shard_map/ppermute | solution.py:43
  66.6 18.0 %copy-start.6 = (s32[4]{0:T(128)S(1)}, s32[4]{0:T(128)}, u32[]{:S(2)}) copy-start(s32[4]{0:T(128)} %param.12) | copy-start | bytes 52
  66.6 18.5 %copy-start.1 = (bf16[128,320]{0,1:T(8,128)(2,1)S(1)}, bf16[128,320]{0,1:T(8,128)(2,1)}, u32[]{:S(2)}) copy-start(bf16[128,320]{0,1:T(8,128)(2,1)} %param.10) | copy-start | bytes 245764
  74.6 23.4 %copy-start = (bf16[1280,320]{0,1:T(8,128)(2,1)S(1)}, bf16[1280,320]{0,1:T(8,128)(2,1)}, u32[]{:S(2)}) copy-start(bf16[1280,320]{0,1:T(8,128)(2,1)} %param.17) | copy-start | bytes 2457604
  74.6 20.9 %collective-permute-start.10 = (bf16[320,512]{1,0:T(8,128)(2,1)}, bf16[320,512]{1,0:T(8,128)(2,1)}, u32[]{:S(2)}, u32[]{:S(2)}) collective-permute-start(bf16[320,512]{1,0:T(8,128)(2,1)} %shard_map.106.own_ref), channel_id=1, source_target_pairs={{0,3},{1,2},{2,1},{3,0},{4,7},{5,6},{6,5},{7,4},{8,11},{9,10},{10,... | collective-permute-start | bytes 983048 | tf_op jit(solution)/shard_map/ppermute | solution.py:43
  78.2 17.2 %collective-permute-start.9 = (bf16[320,512]{1,0:T(8,128)(2,1)}, bf16[320,512]{1,0:T(8,128)(2,1)}, u32[]{:S(2)}, u32[]{:S(2)}) collective-permute-start(bf16[320,512]{1,0:T(8,128)(2,1)} %shard_map.106.own_ref), channel_id=1, source_target_pairs={{0,2},{1,3},{2,0},{3,1},{4,6},{5,7},{6,4},{7,5},{8,10},{9,11},{10,... | collective-permute-start | bytes 983048 | tf_op jit(solution)/shard_map/ppermute | solution.py:43
  81.0 17.0 %collective-permute-start.8 = (bf16[320,512]{1,0:T(8,128)(2,1)}, bf16[320,512]{1,0:T(8,128)(2,1)}, u32[]{:S(2)}, u32[]{:S(2)}) collective-permute-start(bf16[320,512]{1,0:T(8,128)(2,1)} %shard_map.106.own_ref), channel_id=1, source_target_pairs={{0,1},{1,0},{2,3},{3,2},{4,5},{5,4},{6,7},{7,6},{8,9},{9,8},{10,11... | collective-permute-start | bytes 983048 | tf_op jit(solution)/shard_map/ppermute | solution.py:43

commit v3 on v2

--- a/solution.py
+++ b/solution.py
@@ -48,9 +48,25 @@
     return lax.ppermute(block, axis, [(i, i + 1) for i in pairs] + [(i + 1, i) for i in pairs])
 
 
+def behind(block, axis):
+    return lax.ppermute(block, axis, [(i + 1, i) for i in range(1, lax.axis_size(axis) - 1, 2)])
+
+
+def handed(block, axis):
+    return lax.ppermute(block, axis, [(i + 1, i) for i in range(0, lax.axis_size(axis), 2)])
+
+
 def shifted(block, axis, distance):
     devices = range(lax.axis_size(axis))
     return lax.ppermute(block, axis, [(i, i + distance) for i in devices if i + distance in devices])
+
+
+def copies_body(x_ref, out_ref, sems):
+    moves = [pltpu.make_async_copy(x_ref, out_ref.at[n], sems.at[n]) for n in range(4)]
+    for move in moves:
+        move.start()
+    for move in moves:
+        move.wait()
 
 
 def pack_body(pos_ref, near_ref, other_ref, taps_ref, gains_ref, out_ref):
@@ -64,25 +80,18 @@
     out_ref[2 * RIM + KW + 2 :, :] = jnp.zeros((7, out_ref.shape[1]), jnp.float32)
 
 
-def place(dec, blocks, whole_ref, width):
-    for offset, block in blocks:
-        at = pl.multiple_of((dec ^ offset) * width, width)
-        whole_ref[pl.ds(at, width), :] = block[:width, :]
-
-
 def rounded(value):
     return value.astype(jnp.bfloat16).astype(jnp.float32)
 
 
 def front_body(
-    dec_ref, own_ref, b1_ref, b2_ref, b3_ref, pays_ref, w_hbm, q_ref, kv_ref, resid_ref,
-    xall_ref, x_ref, pad_ref, scale_ref, square_ref, whole_ref, turned_ref, norm_ref, pay_ref, w_ref, sem,
+    dec_ref, xall_ref, pays_ref, w_hbm, q_ref, kv_ref, resid_ref,
+    x_ref, pad_ref, scale_ref, square_ref, whole_ref, turned_ref, norm_ref, pay_ref, w_ref, sem,
 ):
-    width, rows = own_ref.shape
+    width, rows = q_ref.shape
     dec = dec_ref[0]
     fetch = pltpu.make_async_copy(w_hbm, w_ref, sem)
     fetch.start()
-    place(dec, [(0, own_ref), (1, b1_ref), (2, b2_ref), (3, b3_ref)], xall_ref, width)
     for n in range(4):
         pay_ref[:, n * width : (n + 1) * width] = pays_ref[n]
     tiles = D // LANES
@@ -129,7 +138,7 @@
         return carry
 
     lax.fori_loop(0, tiles, tile, 0)
-    resid_ref[...] = turned_ref[pl.ds(pl.multiple_of(dec * width, HD), width), :]
+    resid_ref[...] = turned_ref[pl.ds(pl.multiple_of(dec * width, HD), width), :].astype(jnp.bfloat16)
     scale2 = lax.rsqrt(jnp.sum(square_ref[...], axis=1, keepdims=True) / D + EPS)
     for f in range(tiles):
         lanes = slice(f * LANES, (f + 1) * LANES)
@@ -153,67 +162,99 @@
     return lax.dot_general(left, right, (((0,), (0,)), ((), ())), preferred_element_type=jnp.float32)
 
 
-def self_body(pos_ref, q_ref, own_ref, beside_ref, beyond_ref, far_ref, out_ref, left_ref):
+def attend(kind, present, q_ref, kv_ref, state, put):
     width, rows = q_ref.shape
     tile = rows // 2
-    pos = pos_ref[0]
-    left_ref[...] = jnp.where(lax.rem(pos, 2) == 1, beside_ref[...], beyond_ref[...])
-    has_left = pos >= 1
-    has_far = pos >= 2
     j = lax.broadcasted_iota(jnp.int32, (tile, tile), 0)
     i = lax.broadcasted_iota(jnp.int32, (tile, tile), 1)
     after = j > i
-
-    def head(h, carry):
-        at = pl.ds(pl.multiple_of(h * HD, HD), HD)
-        vt = pl.ds(pl.multiple_of(width + h * HD, HD), HD)
+    for h in range(width // HD):
+        at = slice(h * HD, (h + 1) * HD)
+        vt = slice(width + h * HD, width + (h + 1) * HD)
         for part in range(2):
             cols = slice(part * tile, (part + 1) * tile)
+            low, high = (0, tile), (tile, rows)
+            if kind == "own":
+                pieces = [(low, 2)] if part == 0 else [(low, 0), (high, 2)]
+            elif kind == "far":
+                pieces = [(low, 1), (high, 0)] if part == 0 else [(high, 1)]
+            else:
+                pieces = [((0, rows), 0)]
             q = q_ref[at, cols]
-            pieces = [(far_ref, part * tile, (part + 1) * tile, has_far, 1)]
-            if part == 0:
-                pieces.append((far_ref, tile, rows, has_far, 0))
-            pieces.append((left_ref, 0, rows, has_left, 0))
-            if part == 1:
-                pieces.append((own_ref, 0, tile, None, 0))
-            pieces.append((own_ref, part * tile, (part + 1) * tile, None, 2))
             scores = []
             peak = None
-            for ref, lo, hi, present, mask in pieces:
-                s = tdot(ref[at, lo:hi], q)
+            for (lo, hi), mask in pieces:
+                s = tdot(kv_ref[at, lo:hi], q)
                 if mask == 1:
                     s = jnp.where(after, s, -FAR)
                 elif mask == 2:
                     s = jnp.where(after, -FAR, s)
                 top = jnp.max(s, axis=0, keepdims=True)
-                if present is not None:
-                    top = jnp.where(present, top, -FAR)
                 peak = top if peak is None else jnp.maximum(peak, top)
                 scores.append(s)
             peak = peak * LOG2E
             total = None
             acc = None
-            for (ref, lo, hi, present, mask), s in zip(pieces, scores):
-                less = peak if present is None else jnp.where(present, peak, FAR)
+            if state is not None:
+                acc_ref, stat_ref = state
+                old = stat_ref[h : h + 1, cols]
+                peak = jnp.maximum(jnp.where(present, peak, -FAR), old)
+                fade = jnp.exp2(old - peak)
+                total = stat_ref[8 + h : 9 + h, cols] * fade
+                acc = acc_ref[at, cols] * fade
+                less = jnp.where(present, peak, FAR)
+            else:
+                less = peak
+            for ((lo, hi), mask), s in zip(pieces, scores):
                 p = jnp.exp2(s * LOG2E - less)
                 add = jnp.sum(p, axis=0, keepdims=True)
                 total = add if total is None else total + add
-                o = jnp.dot(ref[vt, lo:hi], p.astype(jnp.bfloat16), preferred_element_type=jnp.float32)
+                o = jnp.dot(kv_ref[vt, lo:hi], p.astype(jnp.bfloat16), preferred_element_type=jnp.float32)
                 acc = o if acc is None else acc + o
-            out_ref[at, cols] = (acc / total).astype(jnp.bfloat16)
-        return carry
-
-    lax.fori_loop(0, width // HD, head, 0)
-
-
-def cross_body(pos_ref, q_ref, ends_ref, beside_ref, own_ref, beyond_ref, out_ref):
+            put(h, at, cols, acc, peak, total)
+
+
+def keep_state(acc_ref, stat_ref):
+    def put(h, at, cols, acc, peak, total):
+        acc_ref[at, cols] = acc
+        stat_ref[h : h + 1, cols] = peak
+        stat_ref[8 + h : 9 + h, cols] = total
+
+    return put
+
+
+def own_body(q_ref, kv_ref, acc_ref, stat_ref):
+    attend("own", True, q_ref, kv_ref, None, keep_state(acc_ref, stat_ref))
+
+
+def far_body(pos_ref, q_ref, far_ref, acc_ref, stat_ref, acc_out, stat_out):
+    attend("far", pos_ref[0] >= 2, q_ref, far_ref, (acc_ref, stat_ref), keep_state(acc_out, stat_out))
+
+
+def left_body(pos_ref, q_ref, beside_ref, passed_ref, acc_ref, stat_ref, out_ref, left_ref):
+    pos = pos_ref[0]
+    left_ref[...] = jnp.where(lax.rem(pos, 2) == 1, beside_ref[...], passed_ref[...])
+
+    def put(h, at, cols, acc, peak, total):
+        out_ref[at, cols] = (acc / total).astype(jnp.bfloat16)
+
+    attend("left", pos >= 1, q_ref, left_ref, (acc_ref, stat_ref), put)
+
+
+def cross_body(pos_ref, start_ref, end_ref, q_ref, beside_ref, own_ref, passed_ref, ahead_ref, out_ref, other_ref):
     width, tokens = q_ref.shape
     rows = own_ref.shape[1]
-    first = ends_ref[0:1, :]
-    last = ends_ref[1:2, :]
     pos = pos_ref[0]
-    refs = (beside_ref, own_ref, beyond_ref)
-    places = (pos ^ 1, pos, jnp.where(lax.rem(pos, 2) == 1, pos + 1, pos - 1))
+    odd = lax.rem(pos, 2) == 1
+    other_ref[...] = jnp.where(odd, ahead_ref[...], passed_ref[...])
+    block = lax.broadcasted_iota(jnp.int32, (1, tokens), 1) // TB
+    first = jnp.zeros((1, tokens), jnp.int32)
+    last = jnp.zeros((1, tokens), jnp.int32)
+    for n in range(tokens // TB):
+        first = jnp.where(block == n, start_ref[n] * FB, first)
+        last = jnp.where(block == n, end_ref[n] * FB, last)
+    blocks = (beside_ref, own_ref, other_ref)
+    places = (pos ^ 1, pos, jnp.where(odd, pos + 1, pos - 1))
     keeps = []
     for n in range(3):
         kpos = lax.broadcasted_iota(jnp.int32, (rows, tokens), 0) + places[n] * rows
@@ -223,11 +264,11 @@
         at = slice(h * HD, (h + 1) * HD)
         vt = slice(width + h * HD, width + (h + 1) * HD)
         q = q_ref[at, :] * jnp.bfloat16(SCALE)
-        scores = [jnp.where(keep, tdot(ref[at, :], q), -FAR) for ref, keep in zip(refs, keeps)]
+        scores = [jnp.where(keep, tdot(ref[at, :], q), -FAR) for ref, keep in zip(blocks, keeps)]
         peak = functools.reduce(jnp.maximum, [jnp.max(s, axis=0, keepdims=True) for s in scores]) * LOG2E
         total = None
         acc = None
-        for ref, s in zip(refs, scores):
+        for ref, s in zip(blocks, scores):
             p = jnp.exp2(s * LOG2E - peak)
             add = jnp.sum(p, axis=0, keepdims=True)
             total = add if total is None else total + add
@@ -236,11 +277,13 @@
         out_ref[at, :] = (acc / total).astype(jnp.bfloat16)
 
 
-def out_body(dec_ref, own_ref, b1_ref, b2_ref, b3_ref, w_ref, resid_ref, out_ref, whole_ref):
-    width = own_ref.shape[0]
-    place(dec_ref[0], [(0, own_ref), (1, b1_ref), (2, b2_ref), (3, b3_ref)], whole_ref, width)
+def out_body(dec_ref, b0_ref, b1_ref, b2_ref, b3_ref, w_ref, resid_ref, out_ref, whole_ref):
+    width = out_ref.shape[0]
+    for n, block in zip((0, 1, 3, 2), (b0_ref, b1_ref, b2_ref, b3_ref)):
+        at = pl.multiple_of((dec_ref[0] ^ n) * width, HD)
+        whole_ref[pl.ds(at, width), :] = block[...]
     mixed = jnp.dot(w_ref[...], whole_ref[...], preferred_element_type=jnp.float32)
-    out_ref[...] = (resid_ref[...] + mixed).astype(jnp.bfloat16)
+    out_ref[...] = (resid_ref[...].astype(jnp.float32) + mixed).astype(jnp.bfloat16)
 
 
 def local(frames, queries, align_start, align_end, gain_conv, conv_kernel, gain_attn, w_qkv, w_out):
@@ -256,30 +299,34 @@
     odd = lax.rem(pos[0], 2) == 1
     near = swapped(jnp.where(odd, head, tail), "ctx", 1)
     other = across(jnp.where(odd, tail, head), "ctx")
-    b2, b1, b3 = swapped(x, "dec", 2), swapped(x, "dec", 1), swapped(x, "dec", 3)
+    copies = pl.pallas_call(
+        copies_body,
+        out_shape=sds((4, width, rows), bf16),
+        in_specs=[VMEM],
+        out_specs=HBM,
+        scratch_shapes=[pltpu.SemaphoreType.DMA((4,))],
+        cost_estimate=pl.CostEstimate(flops=0, bytes_accessed=2_000_000, transcendentals=0),
+    )(x)
+    x_all = lax.all_to_all(copies, "dec", 0, 0).reshape(D, rows)
     pay = call(
         pack_body,
         sds((72, width), f32),
         1,
         (pos, near, other, conv_kernel, jnp.stack([gain_conv, gain_attn])),
-        flops=50_000_000_000,
+        flops=1_000_000,
         nbytes=300_000,
     )
-    pay = lax.all_gather(pay, "dec", axis=0)
+    pays = lax.all_gather(pay, "dec", axis=0)
     w_t = jnp.transpose(w_qkv, (1, 2, 0)).reshape(3 * width, D)
     wo_t = w_out.T
-    ends = jnp.stack([jnp.repeat(align_start * FB, TB), jnp.repeat(align_end * FB, TB)], 0)
-    ends = jnp.concatenate([ends, jnp.zeros((6, tokens), jnp.int32)], axis=0)
-
     q, kv, resid = call(
         front_body,
-        (sds((width, rows), bf16), sds((2 * width, rows), bf16), sds((width, rows), f32)),
+        (sds((width, rows), bf16), sds((2 * width, rows), bf16), sds((width, rows), bf16)),
         1,
-        (dec, x, b1, b2, b3, pay, w_t),
+        (dec, x_all, pays, w_t),
         hbm=1,
-        mib=48,
+        mib=50,
         scratch=[
-            pltpu.VMEM((D, rows), bf16),
             pltpu.VMEM((rows, LANES), f32),
             pltpu.VMEM((rows + 3 * RIM, LANES), f32),
             pltpu.VMEM((rows, LANES), f32),
@@ -294,25 +341,31 @@
         flops=2 * 3 * width * D * rows,
         nbytes=5_000_000,
     )
+    beside = swapped(kv, "ctx", 1)
+    ahead = behind(kv, "ctx")
     far = shifted(kv, "ctx", 2)
-    beyond = across(kv, "ctx")
-    beside = swapped(kv, "ctx", 1)
+    state = (sds((width, rows), f32), sds((16, rows), f32))
+    work = dict(flops=4 * width * rows * rows, nbytes=2_500_000, exps=5 * rows * 512)
+    acc, stat = call(own_body, state, 0, (q, kv), **work)
+    beside, ahead, far, acc, stat = lax.optimization_barrier((beside, ahead, far, acc, stat))
+    passed = handed(far, "ctx")
+    acc, stat = call(far_body, state, 1, (pos, q, far, acc, stat), **work)
     attn = call(
-        self_body,
+        left_body,
         sds((width, rows), bf16),
         1,
-        (pos, q, kv, beside, beyond, far),
+        (pos, q, beside, passed, acc, stat),
         scratch=[pltpu.VMEM((2 * width, rows), bf16)],
-        flops=8 * width * rows * 1280,
-        nbytes=2_500_000,
-        exps=5 * rows * 1280,
-    )
-    a2, a1, a3 = swapped(attn, "dec", 2), swapped(attn, "dec", 1), swapped(attn, "dec", 3)
+        **work,
+    )
+    whole = [attn] + [swapped(attn, "dec", bits) for bits in (1, 3, 2)]
+    attn_q, _ = lax.optimization_barrier((queries.T, attn))
     crossed = call(
         cross_body,
         sds((width, tokens), bf16),
-        1,
-        (pos, queries.T, ends, beside, kv, beyond),
+        3,
+        (pos, align_start, align_end, attn_q, beside, kv, passed, ahead),
+        scratch=[pltpu.VMEM((2 * width, rows), bf16)],
         flops=4 * width * tokens * 3 * rows,
         nbytes=2_000_000,
         exps=5 * tokens * 3 * rows,
@@ -321,7 +374,7 @@
         out_body,
         sds((width, rows), bf16),
         1,
-        (dec, attn, a1, a2, a3, wo_t, resid),
+        (dec, *whole, wo_t, resid),
         scratch=[pltpu.VMEM((D, rows), bf16)],
         flops=2 * width * D * rows,
         nbytes=3_500_000,

time: 101 us -> 94.8 us (0.939)
  the two profiles are of different devices: /device:TPU:100 before, /device:TPU:257 now
where the time goes in v3:
time: 94.8 us; the launch traced here: 94.4 us
  starting transfers between devices  35.1 us (37%)
  Pallas kernels  26.4 us (28%)
  blocking collectives  17.1 us (18%)
  waiting for transfers between devices  14.6 us (15%)
    pallas_call x7, Pallas kernels, call(): pl.pallas_call(kernel, out_shape=outs, in_specs=specs, out_specs=jax.tree...  24.4 us
    ppermute x5, starting transfers between devices, swapped(): lax.ppermute(block, axis, [(i, i ^ bits) for i in range(lax.axis_size(axi...  17.4 us
    all_gather x1, blocking collectives, local(): pays = lax.all_gather(pay, 'dec', axis=0)  17.1 us
    ppermute x5, waiting for transfers between devices, swapped(): lax.ppermute(block, axis, [(i, i ^ bits) for i in range(lax.axis_size(axi...  8.52 us
    ppermute x1, waiting for transfers between devices, shifted(): lax.ppermute(block, axis, [(i, i + distance) for i in devices if i + dist...  6.02 us
    ppermute x1, starting transfers between devices, handed(): lax.ppermute(block, axis, [(i + 1, i) for i in range(0, lax.axis_size(axi...  5.01 us
    all_to_all x1, starting transfers between devices, local(): x_all = lax.all_to_all(copies, 'dec', 0, 0).reshape(D, rows)  4.33 us
    ppermute x1, starting transfers between devices, across(): lax.ppermute(block, axis, [(i, i + 1) for i in pairs] + [(i + 1, i) for i...  3.96 us
  transfers between devices with their start and end apart: 10, of which 4 were waited for; matrix products, arithmetic and copies ran while one was open for 0% of the time, Pallas kernels for 9%

profile of v3, /device:TPU:257, one launch (start us, length us, event | category | flops | bytes accessed | tf_op | source)
XLA Modules:
  0.0 94.4 jit_solution(3276489239828761475)
XLA Ops:
  0.6 2.1 %shard_map.104 = bf16[4,320,512]{2,1,0:T(8,128)(2,1)} custom-call(bf16[320,512]{1,0:T(8,128)(2,1)} %bitcast.16), custom_call_target="tpu_custom_call" | custom-call | bytes 2000000 | tf_op jit(solution)/shard_map/pallas_call | solution.py:302
  2.7 0.0 copy-start.5
  2.7 0.0 copy-start.6
  2.7 0.0 copy-start.7
  2.8 0.0 copy-start.2
  2.8 4.3 %all-to-all-start = ((bf16[4,320,512]{2,1,0:T(8,128)(2,1)}), bf16[4,320,512]{2,1,0:T(8,128)(2,1)S(1)}, u32[]{:S(2)}, u32[]{:S(2)}) async-start(bf16[4,320,512]{2,1,0:T(8,128)(2,1)} %shard_map.104), calls=%async_computation | async-start | bytes 2621440 | tf_op jit(solution)/shard_map/all_to_all | solution.py:310
  7.1 0.1 fusion
  7.2 0.1 copy.14
  7.3 0.1 copy.13
  7.4 4.0 %collective-permute-start.1 = (bf16[16,320]{1,0:T(8,128)(2,1)S(1)}, bf16[16,320]{1,0:T(8,128)(2,1)S(1)}, u32[]{:S(2)}, u32[]{:S(2)}) collective-permute-start(bf16[16,320]{1,0:T(8,128)(2,1)S(1)} %get-tuple-element.30), channel_id=1, source_target_pairs={{4,8},{12,16},{20,24},{28,32},{36,40},{44,48},{52,56},{60,64},{68,... | collective-permute-start | bytes 30728 | tf_op jit(solution)/shard_map/ppermute | solution.py:48
  11.3 2.3 %collective-permute-start = (bf16[16,320]{1,0:T(8,128)(2,1)S(1)}, bf16[16,320]{1,0:T(8,128)(2,1)S(1)}, u32[]{:S(2)}, u32[]{:S(2)}) collective-permute-start(bf16[16,320]{1,0:T(8,128)(2,1)S(1)} %get-tuple-element.31), channel_id=1, source_target_pairs={{0,4},{4,0},{8,12},{12,8},{16,20},{20,16},{24,28},{28,24},{32,36},... | collective-permute-start | bytes 30728 | tf_op jit(solution)/shard_map/ppermute | solution.py:43
  13.7 0.7 collective-permute-done.near_ref
  14.5 17.1 %all-gather = f32[288,320]{1,0:T(8,128)S(1)} all-gather(f32[72,320]{1,0:T(8,128)S(1)} %shard_map.105), channel_id=2, replica_groups=mesh['ctx'=128,'dec'=4] {'dec'}, dimensions={0}, use_global_device_ids=true | all-gather | bytes 460800 | tf_op jit(solution)/shard_map/all_gather | solution.py:319
  31.6 10.3 %shard_map.106 = (bf16[320,512]{1,0:T(8,128)(2,1)S(1)}, bf16[640,512]{1,0:T(8,128)(2,1)S(1)}, bf16[320,512]{1,0:T(8,128)(2,1)S(1)}) custom-call(s32[1]{0:T(128)} %bitcast.dec_ref, bf16[1280,512]{1,0:T(8,128)(2,1)S(1)} %bitcast.12, f32[4,72,320]{2,1,0:T(8,128)S(1)} %bitcast.14, bf16[960,1280]{1,0:T(8,128)(2,1)} %bitcast.19), custom_call_target="tpu_custom_call" | custom-call | flops 1258291200 | bytes 5000000 | tf_op jit(solution)/shard_map/pallas_call | solution.py:31
  41.9 3.1 %collective-permute-start.4 = (bf16[640,512]{1,0:T(8,128)(2,1)S(1)}, bf16[640,512]{1,0:T(8,128)(2,1)S(1)}, u32[]{:S(2)}, u32[]{:S(2)}) collective-permute-start(bf16[640,512]{1,0:T(8,128)(2,1)S(1)} %get-tuple-element.16.kv_ref.own_ref), channel_id=1, source_target_pairs={{0,8},{4,12},{8,16},{12,20},{16,24},{20,28},{24,32},{28,36},{32,40... | collective-permute-start | bytes 1966088 | tf_op jit(solution)/shard_map/ppermute | solution.py:61
  45.0 1.3 %collective-permute-start.3 = (bf16[640,512]{1,0:T(8,128)(2,1)S(1)}, bf16[640,512]{1,0:T(8,128)(2,1)S(1)}, u32[]{:S(2)}, u32[]{:S(2)}) collective-permute-start(bf16[640,512]{1,0:T(8,128)(2,1)S(1)} %get-tuple-element.16.kv_ref.own_ref), channel_id=1, source_target_pairs={{8,4},{16,12},{24,20},{32,28},{40,36},{48,44},{56,52},{64,60},{72,... | collective-permute-start | bytes 1966088 | tf_op jit(solution)/shard_map/ppermute | solution.py:52
  46.3 6.5 %collective-permute-start.2 = (bf16[640,512]{1,0:T(8,128)(2,1)S(1)}, bf16[640,512]{1,0:T(8,128)(2,1)S(1)}, u32[]{:S(2)}, u32[]{:S(2)}) collective-permute-start(bf16[640,512]{1,0:T(8,128)(2,1)S(1)} %get-tuple-element.16.kv_ref.own_ref), channel_id=1, source_target_pairs={{0,4},{4,0},{8,12},{12,8},{16,20},{20,16},{24,28},{28,24},{32,36},... | collective-permute-start | bytes 1966088 | tf_op jit(solution)/shard_map/ppermute | solution.py:43
  52.8 2.3 %shard_map.107 = (f32[320,512]{1,0:T(8,128)S(1)}, f32[16,512]{1,0:T(8,128)S(1)}) custom-call(bf16[320,512]{1,0:T(8,128)(2,1)S(1)} %get-tuple-element.15.q_ref, bf16[640,512]{1,0:T(8,128)(2,1)S(1)} %get-tuple-element.16.kv_ref.own_ref), custom_call_target="tpu_custom_call" | custom-call | flops 335544320 | bytes 2500000 | tf_op jit(solution)/shard_map/pallas_call | solution.py:31
  55.1 6.0 %collective-permute-done.4.far_ref = bf16[640,512]{1,0:T(8,128)(2,1)S(1)} collective-permute-done((bf16[640,512]{1,0:T(8,128)(2,1)S(1)}, bf16[640,512]{1,0:T(8,128)(2,1)S(1)}, u32[]{:S(2)}, u32[]{:S(2)}) %collective-permute-start.4) | collective-permute-done | bytes 655392 | tf_op jit(solution)/shard_map/ppermute | solution.py:61
  61.2 5.0 %collective-permute-start.5 = (bf16[640,512]{1,0:T(8,128)(2,1)S(1)}, bf16[640,512]{1,0:T(8,128)(2,1)S(1)}, u32[]{:S(2)}, u32[]{:S(2)}) collective-permute-start(bf16[640,512]{1,0:T(8,128)(2,1)S(1)} %collective-permute-done.4.far_ref), channel_id=1, source_target_pairs={{4,0},{12,8},{20,16},{28,24},{36,32},{44,40},{52,48},{60,56},{68,6... | collective-permute-start | bytes 1966088 | tf_op jit(solution)/shard_map/ppermute | solution.py:56
  66.2 2.2 %shard_map.108 = (f32[320,512]{1,0:T(8,128)S(1)}, f32[16,512]{1,0:T(8,128)S(1)}) custom-call(s32[1]{0:T(128)} %bitcast.1.pos_ref, bf16[320,512]{1,0:T(8,128)(2,1)S(1)} %get-tuple-element.15.q_ref, bf16[640,512]{1,0:T(8,128)(2,1)S(1)} %collective-permute-done.4.far_ref, f32[320,512]{1,0:T(8,128)S(1)} %get-tuple-element.21.acc_ref, ...), custom_call_target="tpu_custom_call" | custom-call | flops 335544320 | bytes 2500000 | tf_op jit(solution)/shard_map/pallas_call | solution.py:31
  68.4 0.0 copy-start.1
  68.4 0.0 copy-start.3
  68.5 4.5 %shard_map.109.b0_ref = bf16[320,512]{1,0:T(8,128)(2,1)S(1)} custom-call(s32[1]{0:T(128)} %bitcast.1.pos_ref, bf16[320,512]{1,0:T(8,128)(2,1)S(1)} %get-tuple-element.15.q_ref, bf16[640,512]{1,0:T(8,128)(2,1)S(1)} %collective-permute-done.2.beside_ref, bf16[640,512]{1,0:T(8,128)(2,1)S(1)} %collective-permute-done.5.passed_ref, ...), custom_call_target="tpu_custom_call" | custom-call | flops 335544320 | bytes 2500000 | tf_op jit(solution)/shard_map/pallas_call | solution.py:31
  72.9 3.4 %collective-permute-start.8 = (bf16[320,512]{1,0:T(8,128)(2,1)S(1)}, bf16[320,512]{1,0:T(8,128)(2,1)S(1)}, u32[]{:S(2)}, u32[]{:S(2)}) collective-permute-start(bf16[320,512]{1,0:T(8,128)(2,1)S(1)} %shard_map.109.b0_ref), channel_id=1, source_target_pairs={{0,2},{1,3},{2,0},{3,1},{4,6},{5,7},{6,4},{7,5},{8,10},{9,11},{10,... | collective-permute-start | bytes 983048 | tf_op jit(solution)/shard_map/ppermute | solution.py:43
  76.3 3.1 %collective-permute-start.7 = (bf16[320,512]{1,0:T(8,128)(2,1)S(1)}, bf16[320,512]{1,0:T(8,128)(2,1)S(1)}, u32[]{:S(2)}, u32[]{:S(2)}) collective-permute-start(bf16[320,512]{1,0:T(8,128)(2,1)S(1)} %shard_map.109.b0_ref), channel_id=1, source_target_pairs={{0,3},{1,2},{2,1},{3,0},{4,7},{5,6},{6,5},{7,4},{8,11},{9,10},{10,... | collective-permute-start | bytes 983048 | tf_op jit(solution)/shard_map/ppermute | solution.py:43
  79.4 2.1 %collective-permute-start.6 = (bf16[320,512]{1,0:T(8,128)(2,1)S(1)}, bf16[320,512]{1,0:T(8,128)(2,1)S(1)}, u32[]{:S(2)}, u32[]{:S(2)}) collective-permute-start(bf16[320,512]{1,0:T(8,128)(2,1)S(1)} %shard_map.109.b0_ref), channel_id=1, source_target_pairs={{0,1},{1,0},{2,3},{3,2},{4,5},{5,4},{6,7},{7,6},{8,9},{9,8},{10,11... | collective-permute-start | bytes 983048 | tf_op jit(solution)/shard_map/ppermute | solution.py:43
  81.5 0.0 copy-start
  81.5 3.7 %shard_map.111 = bf16[320,128]{1,0:T(8,128)(2,1)} custom-call(s32[1]{0:T(128)} %bitcast.1.pos_ref, s32[4]{0:T(128)S(1)} %copy-done.3, s32[4]{0:T(128)S(1)} %copy-done.4, bf16[320,128]{1,0:T(8,128)(2,1)S(1)} %bitcast.15, bf16[640,512]{1,0:T(8,128)(2,1)S(1)} %collective-permute-done.2.beside_ref, bf16[640,512]{1,0:T(8,128)(2,1)S(1)} %get-tuple-element.16.kv_ref.own_ref, ...), custom_call_target="tpu_custom_call" | custom-call | flops 251658240 | bytes 2000000 | tf_op jit(solution)/shard_map/pallas_call | solution.py:31
  85.2 0.6 collective-permute-done.8.b3_ref
  85.9 7.2 %collective-permute-done.7.b2_ref = bf16[320,512]{1,0:T(8,128)(2,1)S(1)} collective-permute-done((bf16[320,512]{1,0:T(8,128)(2,1)S(1)}, bf16[320,512]{1,0:T(8,128)(2,1)S(1)}, u32[]{:S(2)}, u32[]{:S(2)}) %collective-permute-start.7) | collective-permute-done | bytes 327712 | tf_op jit(solution)/shard_map/ppermute | solution.py:43
  93.0 1.4 %shard_map.110 = bf16[320,512]{1,0:T(8,128)(2,1)} custom-call(s32[1]{0:T(128)} %bitcast.dec_ref, bf16[320,512]{1,0:T(8,128)(2,1)S(1)} %shard_map.109.b0_ref, bf16[320,512]{1,0:T(8,128)(2,1)S(1)} %collective-permute-done.6.b1_ref, bf16[320,512]{1,0:T(8,128)(2,1)S(1)} %collective-permute-done.7.b2_ref, bf16[320,512]{1,0:T(8,128)(2,1)S(1)} %collective-permute-done.8.b3_ref, ...), custom_call_target="tpu_custom_call" | custom-call | flops 419430400 | bytes 3500000 | tf_op jit(solution)/shard_map/pallas_call | solution.py:31
  (20 shorter events, 0.1 us)
Async XLA Ops:
  2.7 4.4 %copy-start.5 = (bf16[512,320]{0,1:T(8,128)(2,1)S(1)}, bf16[512,320]{0,1:T(8,128)(2,1)}, u32[]{:S(2)}) copy-start(bf16[512,320]{0,1:T(8,128)(2,1)} %param.9) | copy-start | bytes 983044
  2.7 10.9 %copy-start.6 = (f32[320]{0:T(512)S(1)}, f32[320]{0:T(512)}, u32[]{:S(2)}) copy-start(f32[320]{0:T(512)} %param.13) | copy-start | bytes 3844
  2.7 10.9 %copy-start.7 = (f32[320]{0:T(512)S(1)}, f32[320]{0:T(512)}, u32[]{:S(2)}) copy-start(f32[320]{0:T(512)} %param.15) | copy-start | bytes 3844
  2.8 11.7 %copy-start.2 = (f32[31,320]{1,0:T(8,128)S(1)}, f32[31,320]{1,0:T(8,128)}, u32[]{:S(2)}) copy-start(f32[31,320]{1,0:T(8,128)} %taps_ref.1) | copy-start | bytes 119044
  2.8 28.8 %all-to-all-start = ((bf16[4,320,512]{2,1,0:T(8,128)(2,1)}), bf16[4,320,512]{2,1,0:T(8,128)(2,1)S(1)}, u32[]{:S(2)}, u32[]{:S(2)}) async-start(bf16[4,320,512]{2,1,0:T(8,128)(2,1)} %shard_map.104), calls=%async_computation | async-start | bytes 2621440 | tf_op jit(solution)/shard_map/all_to_all | solution.py:310
  7.4 6.3 %collective-permute-start.1 = (bf16[16,320]{1,0:T(8,128)(2,1)S(1)}, bf16[16,320]{1,0:T(8,128)(2,1)S(1)}, u32[]{:S(2)}, u32[]{:S(2)}) collective-permute-start(bf16[16,320]{1,0:T(8,128)(2,1)S(1)} %get-tuple-element.30), channel_id=1, source_target_pairs={{4,8},{12,16},{20,24},{28,32},{36,40},{44,48},{52,56},{60,64},{68,... | collective-permute-start | bytes 30728 | tf_op jit(solution)/shard_map/ppermute | solution.py:48
  11.3 3.1 %collective-permute-start = (bf16[16,320]{1,0:T(8,128)(2,1)S(1)}, bf16[16,320]{1,0:T(8,128)(2,1)S(1)}, u32[]{:S(2)}, u32[]{:S(2)}) collective-permute-start(bf16[16,320]{1,0:T(8,128)(2,1)S(1)} %get-tuple-element.31), channel_id=1, source_target_pairs={{0,4},{4,0},{8,12},{12,8},{16,20},{20,16},{24,28},{28,24},{32,36},... | collective-permute-start | bytes 30728 | tf_op jit(solution)/shard_map/ppermute | solution.py:43
  41.9 19.3 %collective-permute-start.4 = (bf16[640,512]{1,0:T(8,128)(2,1)S(1)}, bf16[640,512]{1,0:T(8,128)(2,1)S(1)}, u32[]{:S(2)}, u32[]{:S(2)}) collective-permute-start(bf16[640,512]{1,0:T(8,128)(2,1)S(1)} %get-tuple-element.16.kv_ref.own_ref), channel_id=1, source_target_pairs={{0,8},{4,12},{8,16},{12,20},{16,24},{20,28},{24,32},{28,36},{32,40... | collective-permute-start | bytes 1966088 | tf_op jit(solution)/shard_map/ppermute | solution.py:61
  45.0 16.2 %collective-permute-start.3 = (bf16[640,512]{1,0:T(8,128)(2,1)S(1)}, bf16[640,512]{1,0:T(8,128)(2,1)S(1)}, u32[]{:S(2)}, u32[]{:S(2)}) collective-permute-start(bf16[640,512]{1,0:T(8,128)(2,1)S(1)} %get-tuple-element.16.kv_ref.own_ref), channel_id=1, source_target_pairs={{8,4},{16,12},{24,20},{32,28},{40,36},{48,44},{56,52},{64,60},{72,... | collective-permute-start | bytes 1966088 | tf_op jit(solution)/shard_map/ppermute | solution.py:52
  46.3 14.9 %collective-permute-start.2 = (bf16[640,512]{1,0:T(8,128)(2,1)S(1)}, bf16[640,512]{1,0:T(8,128)(2,1)S(1)}, u32[]{:S(2)}, u32[]{:S(2)}) collective-permute-start(bf16[640,512]{1,0:T(8,128)(2,1)S(1)} %get-tuple-element.16.kv_ref.own_ref), channel_id=1, source_target_pairs={{0,4},{4,0},{8,12},{12,8},{16,20},{20,16},{24,28},{28,24},{32,36},... | collective-permute-start | bytes 1966088 | tf_op jit(solution)/shard_map/ppermute | solution.py:43
  61.2 7.2 %collective-permute-start.5 = (bf16[640,512]{1,0:T(8,128)(2,1)S(1)}, bf16[640,512]{1,0:T(8,128)(2,1)S(1)}, u32[]{:S(2)}, u32[]{:S(2)}) collective-permute-start(bf16[640,512]{1,0:T(8,128)(2,1)S(1)} %collective-permute-done.4.far_ref), channel_id=1, source_target_pairs={{4,0},{12,8},{20,16},{28,24},{36,32},{44,40},{52,48},{60,56},{68,6... | collective-permute-start | bytes 1966088 | tf_op jit(solution)/shard_map/ppermute | solution.py:56
  68.4 13.1 %copy-start.1 = (bf16[128,320]{0,1:T(8,128)(2,1)S(1)}, bf16[128,320]{0,1:T(8,128)(2,1)}, u32[]{:S(2)}) copy-start(bf16[128,320]{0,1:T(8,128)(2,1)} %param.10) | copy-start | bytes 245764
  68.4 13.1 %copy-start.3 = (s32[4]{0:T(128)S(1)}, s32[4]{0:T(128)}, u32[]{:S(2)}) copy-start(s32[4]{0:T(128)} %start_ref.1) | copy-start | bytes 52
  68.4 13.1 %copy-start.4 = (s32[4]{0:T(128)S(1)}, s32[4]{0:T(128)}, u32[]{:S(2)}) copy-start(s32[4]{0:T(128)} %end_ref.1) | copy-start | bytes 52
  72.9 12.9 %collective-permute-start.8 = (bf16[320,512]{1,0:T(8,128)(2,1)S(1)}, bf16[320,512]{1,0:T(8,128)(2,1)S(1)}, u32[]{:S(2)}, u32[]{:S(2)}) collective-permute-start(bf16[320,512]{1,0:T(8,128)(2,1)S(1)} %shard_map.109.b0_ref), channel_id=1, source_target_pairs={{0,2},{1,3},{2,0},{3,1},{4,6},{5,7},{6,4},{7,5},{8,10},{9,11},{10,... | collective-permute-start | bytes 983048 | tf_op jit(solution)/shard_map/ppermute | solution.py:43
  76.3 16.7 %collective-permute-start.7 = (bf16[320,512]{1,0:T(8,128)(2,1)S(1)}, bf16[320,512]{1,0:T(8,128)(2,1)S(1)}, u32[]{:S(2)}, u32[]{:S(2)}) collective-permute-start(bf16[320,512]{1,0:T(8,128)(2,1)S(1)} %shard_map.109.b0_ref), channel_id=1, source_target_pairs={{0,3},{1,2},{2,1},{3,0},{4,7},{5,6},{6,5},{7,4},{8,11},{9,10},{10,... | collective-permute-start | bytes 983048 | tf_op jit(solution)/shard_map/ppermute | solution.py:43
  79.4 13.6 %collective-permute-start.6 = (bf16[320,512]{1,0:T(8,128)(2,1)S(1)}, bf16[320,512]{1,0:T(8,128)(2,1)S(1)}, u32[]{:S(2)}, u32[]{:S(2)}) collective-permute-start(bf16[320,512]{1,0:T(8,128)(2,1)S(1)} %shard_map.109.b0_ref), channel_id=1, source_target_pairs={{0,1},{1,0},{2,3},{3,2},{4,5},{5,4},{6,7},{7,6},{8,9},{9,8},{10,11... | collective-permute-start | bytes 983048 | tf_op jit(solution)/shard_map/ppermute | solution.py:43
  81.5 11.5 %copy-start = (bf16[1280,320]{0,1:T(8,128)(2,1)S(1)}, bf16[1280,320]{0,1:T(8,128)(2,1)}, u32[]{:S(2)}) copy-start(bf16[1280,320]{0,1:T(8,128)(2,1)} %param.17) | copy-start | bytes 2457604

commit v4 on v3

--- a/solution.py
+++ b/solution.py
@@ -61,12 +61,9 @@
     return lax.ppermute(block, axis, [(i, i + distance) for i in devices if i + distance in devices])
 
 
-def copies_body(x_ref, out_ref, sems):
-    moves = [pltpu.make_async_copy(x_ref, out_ref.at[n], sems.at[n]) for n in range(4)]
-    for move in moves:
-        move.start()
-    for move in moves:
-        move.wait()
+def copies_body(x_ref, out_ref):
+    for n in range(4):
+        out_ref[n] = x_ref[...]
 
 
 def pack_body(pos_ref, near_ref, other_ref, taps_ref, gains_ref, out_ref):
@@ -86,7 +83,7 @@
 
 def front_body(
     dec_ref, xall_ref, pays_ref, w_hbm, q_ref, kv_ref, resid_ref,
-    x_ref, pad_ref, scale_ref, square_ref, whole_ref, turned_ref, norm_ref, pay_ref, w_ref, sem,
+    x0_ref, pad0_ref, x1_ref, pad1_ref, scale_ref, square_ref, whole_ref, turned_ref, norm_ref, pay_ref, w_ref, sem,
 ):
     width, rows = q_ref.shape
     dec = dec_ref[0]
@@ -109,7 +106,7 @@
     square_ref[...] = jnp.zeros_like(square_ref)
     strip = 64
 
-    def tile(f, carry):
+    def prepare(f, x_ref, pad_ref):
         lanes = pl.ds(pl.multiple_of(f * LANES, LANES), LANES)
         gain = pay_ref[2 * RIM + KW : 2 * RIM + KW + 1, lanes]
         x_ref[...] = xall_ref[lanes, :].astype(jnp.float32).T
@@ -117,6 +114,9 @@
         pad_ref[0:RIM, :] = rim[:RIM]
         pad_ref[RIM + rows : 2 * RIM + rows, :] = rim[RIM:]
         pad_ref[RIM : RIM + rows, :] = rounded(x_ref[...] * scale_ref[...] * gain)
+
+    def convolve(f, x_ref, pad_ref):
+        lanes = pl.ds(pl.multiple_of(f * LANES, LANES), LANES)
         for t in range(0, rows, strip):
             conv = None
             for b in range(8):
@@ -131,14 +131,20 @@
             whole_ref[f, t : t + strip, :] = resid
             square_ref[t : t + strip, :] += resid * resid
 
-        @pl.when((f * LANES < (dec + 1) * width) & ((f + 1) * LANES > dec * width))
-        def _():
-            turned_ref[lanes, :] = whole_ref[f].T
-
+    def two_tiles(n, carry):
+        prepare(2 * n + 1, x1_ref, pad1_ref)
+        convolve(2 * n, x0_ref, pad0_ref)
+        prepare(jnp.minimum(2 * n + 2, tiles - 1), x0_ref, pad0_ref)
+        convolve(2 * n + 1, x1_ref, pad1_ref)
         return carry
 
-    lax.fori_loop(0, tiles, tile, 0)
-    resid_ref[...] = turned_ref[pl.ds(pl.multiple_of(dec * width, HD), width), :].astype(jnp.bfloat16)
+    prepare(0, x0_ref, pad0_ref)
+    lax.fori_loop(0, tiles // 2, two_tiles, 0)
+    begin = (dec * width) // LANES
+    for n in range(3):
+        turned_ref[n * LANES : (n + 1) * LANES, :] = whole_ref[begin + n].T
+    offset = pl.multiple_of(dec * width - begin * LANES, HD)
+    resid_ref[...] = turned_ref[pl.ds(offset, width), :].astype(jnp.bfloat16)
     scale2 = lax.rsqrt(jnp.sum(square_ref[...], axis=1, keepdims=True) / D + EPS)
     for f in range(tiles):
         lanes = slice(f * LANES, (f + 1) * LANES)
@@ -164,54 +170,57 @@
 
 def attend(kind, present, q_ref, kv_ref, state, put):
     width, rows = q_ref.shape
-    tile = rows // 2
-    j = lax.broadcasted_iota(jnp.int32, (tile, tile), 0)
-    i = lax.broadcasted_iota(jnp.int32, (tile, tile), 1)
-    after = j > i
+    half = rows // 2
+    j = lax.broadcasted_iota(jnp.int32, (half, rows), 0)
+    i = lax.broadcasted_iota(jnp.int32, (half, rows), 1)
+    if kind == "own":
+        pieces = [((0, half), (0, rows), j > i), ((half, rows), (half, rows), (j > i)[:, :half])]
+    elif kind == "far":
+        pieces = [((half, rows), (0, rows), j + half <= i), ((0, half), (0, half), (j <= i)[:, :half])]
+    else:
+        pieces = [((0, rows), (0, rows), None)]
     for h in range(width // HD):
         at = slice(h * HD, (h + 1) * HD)
         vt = slice(width + h * HD, width + (h + 1) * HD)
-        for part in range(2):
-            cols = slice(part * tile, (part + 1) * tile)
-            low, high = (0, tile), (tile, rows)
-            if kind == "own":
-                pieces = [(low, 2)] if part == 0 else [(low, 0), (high, 2)]
-            elif kind == "far":
-                pieces = [(low, 1), (high, 0)] if part == 0 else [(high, 1)]
-            else:
-                pieces = [((0, rows), 0)]
-            q = q_ref[at, cols]
-            scores = []
-            peak = None
-            for (lo, hi), mask in pieces:
-                s = tdot(kv_ref[at, lo:hi], q)
-                if mask == 1:
-                    s = jnp.where(after, s, -FAR)
-                elif mask == 2:
-                    s = jnp.where(after, -FAR, s)
-                top = jnp.max(s, axis=0, keepdims=True)
-                peak = top if peak is None else jnp.maximum(peak, top)
-                scores.append(s)
-            peak = peak * LOG2E
-            total = None
-            acc = None
-            if state is not None:
-                acc_ref, stat_ref = state
-                old = stat_ref[h : h + 1, cols]
-                peak = jnp.maximum(jnp.where(present, peak, -FAR), old)
-                fade = jnp.exp2(old - peak)
-                total = stat_ref[8 + h : 9 + h, cols] * fade
-                acc = acc_ref[at, cols] * fade
-                less = jnp.where(present, peak, FAR)
-            else:
-                less = peak
-            for ((lo, hi), mask), s in zip(pieces, scores):
-                p = jnp.exp2(s * LOG2E - less)
-                add = jnp.sum(p, axis=0, keepdims=True)
-                total = add if total is None else total + add
-                o = jnp.dot(kv_ref[vt, lo:hi], p.astype(jnp.bfloat16), preferred_element_type=jnp.float32)
-                acc = o if acc is None else acc + o
-            put(h, at, cols, acc, peak, total)
+        scores = []
+        peaks = [None, None]
+        for (lo, hi), (first, last), drop in pieces:
+            s = tdot(kv_ref[at, lo:hi], q_ref[at, first:last])
+            if drop is not None:
+                s = jnp.where(drop, -FAR, s)
+            top = jnp.max(s, axis=0, keepdims=True)
+            for side in range(2):
+                if first <= side * half < last:
+                    part = top[:, side * half - first : side * half - first + half]
+                    peaks[side] = part if peaks[side] is None else jnp.maximum(peaks[side], part)
+            scores.append(s)
+        peak = jnp.concatenate(peaks, axis=1) * LOG2E
+        if state is not None:
+            acc_ref, stat_ref = state
+            old = stat_ref[h : h + 1, :]
+            peak = jnp.maximum(jnp.where(present, peak, -FAR), old)
+            fade = jnp.exp2(old - peak)
+            total = stat_ref[8 + h : 9 + h, :] * fade
+            acc = acc_ref[at, :] * fade
+            less = jnp.where(present, peak, FAR)
+            totals = [total[:, :half], total[:, half:]]
+            accs = [acc[:, :half], acc[:, half:]]
+        else:
+            less = peak
+            totals = [None, None]
+            accs = [None, None]
+        for ((lo, hi), (first, last), _), s in zip(pieces, scores):
+            p = jnp.exp2(s * LOG2E - less[:, first:last])
+            add = jnp.sum(p, axis=0, keepdims=True)
+            o = jnp.dot(kv_ref[vt, lo:hi], p.astype(jnp.bfloat16), preferred_element_type=jnp.float32)
+            for side in range(2):
+                if first <= side * half < last:
+                    cut = slice(side * half - first, side * half - first + half)
+                    totals[side] = add[:, cut] if totals[side] is None else totals[side] + add[:, cut]
+                    accs[side] = o[:, cut] if accs[side] is None else accs[side] + o[:, cut]
+        for side in range(2):
+            cols = slice(side * half, (side + 1) * half)
+            put(h, at, cols, accs[side], peak[:, cols], totals[side])
 
 
 def keep_state(acc_ref, stat_ref):
@@ -299,14 +308,7 @@
     odd = lax.rem(pos[0], 2) == 1
     near = swapped(jnp.where(odd, head, tail), "ctx", 1)
     other = across(jnp.where(odd, tail, head), "ctx")
-    copies = pl.pallas_call(
-        copies_body,
-        out_shape=sds((4, width, rows), bf16),
-        in_specs=[VMEM],
-        out_specs=HBM,
-        scratch_shapes=[pltpu.SemaphoreType.DMA((4,))],
-        cost_estimate=pl.CostEstimate(flops=0, bytes_accessed=2_000_000, transcendentals=0),
-    )(x)
+    copies = call(copies_body, sds((4, width, rows), bf16), 0, (x,), nbytes=2_000_000)
     x_all = lax.all_to_all(copies, "dec", 0, 0).reshape(D, rows)
     pay = call(
         pack_body,
@@ -330,9 +332,11 @@
             pltpu.VMEM((rows, LANES), f32),
             pltpu.VMEM((rows + 3 * RIM, LANES), f32),
             pltpu.VMEM((rows, LANES), f32),
+            pltpu.VMEM((rows + 3 * RIM, LANES), f32),
+            pltpu.VMEM((rows, LANES), f32),
             pltpu.VMEM((rows, LANES), f32),
             pltpu.VMEM((D // LANES, rows, LANES), f32),
-            pltpu.VMEM((D, rows), f32),
+            pltpu.VMEM((3 * LANES, rows), f32),
             pltpu.VMEM((rows, D), bf16),
             pltpu.VMEM((72, D), f32),
             pltpu.VMEM((3 * width, D), bf16),

time: 94.8 us -> 92.2 us (0.973)
  Pallas kernels: 26.4 us -> 22.7 us
  local copies, waits for them, and re-layouts: 0.32 us -> 1.27 us
    pallas_call x1 -> x0, Pallas kernels: 2.08 us -> none  [local(): pl.pallas_call(copies_body, out_shape=sds((4, width, rows), bf16), in_spe...]
    pallas_call x7 -> x8, Pallas kernels: 24.4 us -> 22.7 us  [call(): pl.pallas_call(kernel, out_shape=outs, in_specs=specs, out_specs=jax.tree...]
    unnamed x18 -> x20, local copies, waits for them, and re-layouts: 0.22 us -> 1.17 us
where the time goes in v4:
time: 92.2 us; the launch traced here: 91.8 us
  starting transfers between devices  35.1 us (38%)
  Pallas kernels  22.7 us (25%)
  blocking collectives  17.1 us (19%)
  waiting for transfers between devices  14.7 us (16%)
  local copies, waits for them, and re-layouts  1.27 us (1%)
    pallas_call x8, Pallas kernels, call(): pl.pallas_call(kernel, out_shape=outs, in_specs=specs, out_specs=jax.tree...  22.7 us
    ppermute x5, starting transfers between devices, swapped(): lax.ppermute(block, axis, [(i, i ^ bits) for i in range(lax.axis_size(axi...  17.4 us
    all_gather x1, blocking collectives, local(): pays = lax.all_gather(pay, 'dec', axis=0)  17.1 us
    ppermute x5, waiting for transfers between devices, swapped(): lax.ppermute(block, axis, [(i, i ^ bits) for i in range(lax.axis_size(axi...  8.43 us
    ppermute x1, waiting for transfers between devices, shifted(): lax.ppermute(block, axis, [(i, i + distance) for i in devices if i + dist...  6.29 us
    ppermute x1, starting transfers between devices, handed(): lax.ppermute(block, axis, [(i + 1, i) for i in range(0, lax.axis_size(axi...  5.01 us
    all_to_all x1, starting transfers between devices, local(): x_all = lax.all_to_all(copies, 'dec', 0, 0).reshape(D, rows)  4.33 us
    ppermute x1, starting transfers between devices, across(): lax.ppermute(block, axis, [(i, i + 1) for i in pairs] + [(i + 1, i) for i...  3.96 us
  transfers between devices with their start and end apart: 10, of which 4 were waited for; matrix products, arithmetic and copies ran while one was open for 0% of the time, Pallas kernels for 9%

profile of v4, /device:TPU:257, one launch (start us, length us, event | category | flops | bytes accessed | tf_op | source)
XLA Modules:
  0.0 91.8 jit_solution(2007255755349320248)
XLA Ops:
  0.6 0.0 copy-start.1
  0.6 1.0 %copy-done.1 = bf16[512,320]{0,1:T(8,128)(2,1)S(1)} copy-done((bf16[512,320]{0,1:T(8,128)(2,1)S(1)}, bf16[512,320]{0,1:T(8,128)(2,1)}, u32[]{:S(2)}) %copy-start.1) | copy-done | bytes 327704
  1.6 1.1 %shard_map.104 = bf16[4,320,512]{2,1,0:T(8,128)(2,1)} custom-call(bf16[320,512]{1,0:T(8,128)(2,1)S(1)} %bitcast.14), custom_call_target="tpu_custom_call" | custom-call | bytes 2000000 | tf_op jit(solution)/shard_map/pallas_call | solution.py:31
  2.8 4.3 %all-to-all-start = ((bf16[4,320,512]{2,1,0:T(8,128)(2,1)}), bf16[4,320,512]{2,1,0:T(8,128)(2,1)S(1)}, u32[]{:S(2)}, u32[]{:S(2)}) async-start(bf16[4,320,512]{2,1,0:T(8,128)(2,1)} %shard_map.104), calls=%async_computation | async-start | bytes 2621440 | tf_op jit(solution)/shard_map/all_to_all | solution.py:312
  7.1 0.1 fusion
  7.2 0.1 copy.14
  7.3 0.1 copy.13
  7.4 4.0 %collective-permute-start.1 = (bf16[16,320]{1,0:T(8,128)(2,1)S(1)}, bf16[16,320]{1,0:T(8,128)(2,1)S(1)}, u32[]{:S(2)}, u32[]{:S(2)}) collective-permute-start(bf16[16,320]{1,0:T(8,128)(2,1)S(1)} %get-tuple-element.30), channel_id=1, source_target_pairs={{4,8},{12,16},{20,24},{28,32},{36,40},{44,48},{52,56},{60,64},{68,... | collective-permute-start | bytes 30728 | tf_op jit(solution)/shard_map/ppermute | solution.py:48
  11.3 2.3 %collective-permute-start = (bf16[16,320]{1,0:T(8,128)(2,1)S(1)}, bf16[16,320]{1,0:T(8,128)(2,1)S(1)}, u32[]{:S(2)}, u32[]{:S(2)}) collective-permute-start(bf16[16,320]{1,0:T(8,128)(2,1)S(1)} %get-tuple-element.31), channel_id=1, source_target_pairs={{0,4},{4,0},{8,12},{12,8},{16,20},{20,16},{24,28},{28,24},{32,36},... | collective-permute-start | bytes 30728 | tf_op jit(solution)/shard_map/ppermute | solution.py:43
  13.7 0.7 collective-permute-done.near_ref
  14.5 17.1 %all-gather = f32[288,320]{1,0:T(8,128)S(1)} all-gather(f32[72,320]{1,0:T(8,128)S(1)} %shard_map.105), channel_id=2, replica_groups=mesh['ctx'=128,'dec'=4] {'dec'}, dimensions={0}, use_global_device_ids=true | all-gather | bytes 460800 | tf_op jit(solution)/shard_map/all_gather | solution.py:321
  31.6 9.4 %shard_map.106 = (bf16[320,512]{1,0:T(8,128)(2,1)S(1)}, bf16[640,512]{1,0:T(8,128)(2,1)S(1)}, bf16[320,512]{1,0:T(8,128)(2,1)S(1)}) custom-call(s32[1]{0:T(128)} %bitcast.dec_ref, bf16[1280,512]{1,0:T(8,128)(2,1)S(1)} %bitcast.12, f32[4,72,320]{2,1,0:T(8,128)S(1)} %bitcast.15, bf16[960,1280]{1,0:T(8,128)(2,1)} %bitcast.19), custom_call_target="tpu_custom_call" | custom-call | flops 1258291200 | bytes 5000000 | tf_op jit(solution)/shard_map/pallas_call | solution.py:31
  41.0 3.1 %collective-permute-start.4 = (bf16[640,512]{1,0:T(8,128)(2,1)S(1)}, bf16[640,512]{1,0:T(8,128)(2,1)S(1)}, u32[]{:S(2)}, u32[]{:S(2)}) collective-permute-start(bf16[640,512]{1,0:T(8,128)(2,1)S(1)} %get-tuple-element.16.kv_ref.own_ref), channel_id=1, source_target_pairs={{0,8},{4,12},{8,16},{12,20},{16,24},{20,28},{24,32},{28,36},{32,40... | collective-permute-start | bytes 1966088 | tf_op jit(solution)/shard_map/ppermute | solution.py:61
  44.1 1.3 %collective-permute-start.3 = (bf16[640,512]{1,0:T(8,128)(2,1)S(1)}, bf16[640,512]{1,0:T(8,128)(2,1)S(1)}, u32[]{:S(2)}, u32[]{:S(2)}) collective-permute-start(bf16[640,512]{1,0:T(8,128)(2,1)S(1)} %get-tuple-element.16.kv_ref.own_ref), channel_id=1, source_target_pairs={{8,4},{16,12},{24,20},{32,28},{40,36},{48,44},{56,52},{64,60},{72,... | collective-permute-start | bytes 1966088 | tf_op jit(solution)/shard_map/ppermute | solution.py:52
  45.4 6.5 %collective-permute-start.2 = (bf16[640,512]{1,0:T(8,128)(2,1)S(1)}, bf16[640,512]{1,0:T(8,128)(2,1)S(1)}, u32[]{:S(2)}, u32[]{:S(2)}) collective-permute-start(bf16[640,512]{1,0:T(8,128)(2,1)S(1)} %get-tuple-element.16.kv_ref.own_ref), channel_id=1, source_target_pairs={{0,4},{4,0},{8,12},{12,8},{16,20},{20,16},{24,28},{28,24},{32,36},... | collective-permute-start | bytes 1966088 | tf_op jit(solution)/shard_map/ppermute | solution.py:43
  52.0 2.0 %shard_map.107 = (f32[320,512]{1,0:T(8,128)S(1)}, f32[16,512]{1,0:T(8,128)S(1)}) custom-call(bf16[320,512]{1,0:T(8,128)(2,1)S(1)} %get-tuple-element.15.q_ref, bf16[640,512]{1,0:T(8,128)(2,1)S(1)} %get-tuple-element.16.kv_ref.own_ref), custom_call_target="tpu_custom_call" | custom-call | flops 335544320 | bytes 2500000 | tf_op jit(solution)/shard_map/pallas_call | solution.py:31
  54.0 6.3 %collective-permute-done.4.far_ref = bf16[640,512]{1,0:T(8,128)(2,1)S(1)} collective-permute-done((bf16[640,512]{1,0:T(8,128)(2,1)S(1)}, bf16[640,512]{1,0:T(8,128)(2,1)S(1)}, u32[]{:S(2)}, u32[]{:S(2)}) %collective-permute-start.4) | collective-permute-done | bytes 655392 | tf_op jit(solution)/shard_map/ppermute | solution.py:61
  60.3 0.0 collective-permute-done.3.ahead_ref
  60.3 5.0 %collective-permute-start.5 = (bf16[640,512]{1,0:T(8,128)(2,1)S(1)}, bf16[640,512]{1,0:T(8,128)(2,1)S(1)}, u32[]{:S(2)}, u32[]{:S(2)}) collective-permute-start(bf16[640,512]{1,0:T(8,128)(2,1)S(1)} %collective-permute-done.4.far_ref), channel_id=1, source_target_pairs={{4,0},{12,8},{20,16},{28,24},{36,32},{44,40},{52,48},{60,56},{68,6... | collective-permute-start | bytes 1966088 | tf_op jit(solution)/shard_map/ppermute | solution.py:56
  65.3 2.1 %shard_map.108 = (f32[320,512]{1,0:T(8,128)S(1)}, f32[16,512]{1,0:T(8,128)S(1)}) custom-call(s32[1]{0:T(128)} %bitcast.1.pos_ref, bf16[320,512]{1,0:T(8,128)(2,1)S(1)} %get-tuple-element.15.q_ref, bf16[640,512]{1,0:T(8,128)(2,1)S(1)} %collective-permute-done.4.far_ref, f32[320,512]{1,0:T(8,128)S(1)} %get-tuple-element.21.acc_ref, ...), custom_call_target="tpu_custom_call" | custom-call | flops 335544320 | bytes 2500000 | tf_op jit(solution)/shard_map/pallas_call | solution.py:31
  67.4 0.0 copy-start.3
  67.4 0.0 copy-start.5
  67.4 0.0 copy-start.6
  67.4 2.8 %shard_map.109.b0_ref = bf16[320,512]{1,0:T(8,128)(2,1)S(1)} custom-call(s32[1]{0:T(128)} %bitcast.1.pos_ref, bf16[320,512]{1,0:T(8,128)(2,1)S(1)} %get-tuple-element.15.q_ref, bf16[640,512]{1,0:T(8,128)(2,1)S(1)} %collective-permute-done.2.beside_ref, bf16[640,512]{1,0:T(8,128)(2,1)S(1)} %collective-permute-done.5.passed_ref, ...), custom_call_target="tpu_custom_call" | custom-call | flops 335544320 | bytes 2500000 | tf_op jit(solution)/shard_map/pallas_call | solution.py:31
  70.3 3.4 %collective-permute-start.8 = (bf16[320,512]{1,0:T(8,128)(2,1)S(1)}, bf16[320,512]{1,0:T(8,128)(2,1)S(1)}, u32[]{:S(2)}, u32[]{:S(2)}) collective-permute-start(bf16[320,512]{1,0:T(8,128)(2,1)S(1)} %shard_map.109.b0_ref), channel_id=1, source_target_pairs={{0,2},{1,3},{2,0},{3,1},{4,6},{5,7},{6,4},{7,5},{8,10},{9,11},{10,... | collective-permute-start | bytes 983048 | tf_op jit(solution)/shard_map/ppermute | solution.py:43
  73.6 3.1 %collective-permute-start.7 = (bf16[320,512]{1,0:T(8,128)(2,1)S(1)}, bf16[320,512]{1,0:T(8,128)(2,1)S(1)}, u32[]{:S(2)}, u32[]{:S(2)}) collective-permute-start(bf16[320,512]{1,0:T(8,128)(2,1)S(1)} %shard_map.109.b0_ref), channel_id=1, source_target_pairs={{0,3},{1,2},{2,1},{3,0},{4,7},{5,6},{6,5},{7,4},{8,11},{9,10},{10,... | collective-permute-start | bytes 983048 | tf_op jit(solution)/shard_map/ppermute | solution.py:43
  76.8 2.1 %collective-permute-start.6 = (bf16[320,512]{1,0:T(8,128)(2,1)S(1)}, bf16[320,512]{1,0:T(8,128)(2,1)S(1)}, u32[]{:S(2)}, u32[]{:S(2)}) collective-permute-start(bf16[320,512]{1,0:T(8,128)(2,1)S(1)} %shard_map.109.b0_ref), channel_id=1, source_target_pairs={{0,1},{1,0},{2,3},{3,2},{4,5},{5,4},{6,7},{7,6},{8,9},{9,8},{10,11... | collective-permute-start | bytes 983048 | tf_op jit(solution)/shard_map/ppermute | solution.py:43
  78.9 0.0 copy-start
  78.9 3.8 %shard_map.111 = bf16[320,128]{1,0:T(8,128)(2,1)} custom-call(s32[1]{0:T(128)} %bitcast.1.pos_ref, s32[4]{0:T(128)S(1)} %copy-done.5, s32[4]{0:T(128)S(1)} %copy-done.6, bf16[320,128]{1,0:T(8,128)(2,1)S(1)} %bitcast.16, bf16[640,512]{1,0:T(8,128)(2,1)S(1)} %collective-permute-done.2.beside_ref, bf16[640,512]{1,0:T(8,128)(2,1)S(1)} %get-tuple-element.16.kv_ref.own_ref, ...), custom_call_target="tpu_custom_call" | custom-call | flops 251658240 | bytes 2000000 | tf_op jit(solution)/shard_map/pallas_call | solution.py:31
  82.7 0.5 collective-permute-done.8.b3_ref
  83.1 7.2 %collective-permute-done.7.b2_ref = bf16[320,512]{1,0:T(8,128)(2,1)S(1)} collective-permute-done((bf16[320,512]{1,0:T(8,128)(2,1)S(1)}, bf16[320,512]{1,0:T(8,128)(2,1)S(1)}, u32[]{:S(2)}, u32[]{:S(2)}) %collective-permute-start.7) | collective-permute-done | bytes 327712 | tf_op jit(solution)/shard_map/ppermute | solution.py:43
  90.4 1.4 %shard_map.110 = bf16[320,512]{1,0:T(8,128)(2,1)} custom-call(s32[1]{0:T(128)} %bitcast.dec_ref, bf16[320,512]{1,0:T(8,128)(2,1)S(1)} %shard_map.109.b0_ref, bf16[320,512]{1,0:T(8,128)(2,1)S(1)} %collective-permute-done.6.b1_ref, bf16[320,512]{1,0:T(8,128)(2,1)S(1)} %collective-permute-done.7.b2_ref, bf16[320,512]{1,0:T(8,128)(2,1)S(1)} %collective-permute-done.8.b3_ref, ...), custom_call_target="tpu_custom_call" | custom-call | flops 419430400 | bytes 3500000 | tf_op jit(solution)/shard_map/pallas_call | solution.py:31
  (22 shorter events, 0.1 us)
Async XLA Ops:
  0.6 1.0 %copy-start.1 = (bf16[512,320]{0,1:T(8,128)(2,1)S(1)}, bf16[512,320]{0,1:T(8,128)(2,1)}, u32[]{:S(2)}) copy-start(bf16[512,320]{0,1:T(8,128)(2,1)} %param.9) | copy-start | bytes 983044
  2.8 4.3 %copy-start.2 = (bf16[512,320]{0,1:T(8,128)(2,1)S(1)}, bf16[512,320]{0,1:T(8,128)(2,1)}, u32[]{:S(2)}) copy-start(bf16[512,320]{0,1:T(8,128)(2,1)} %param.9) | copy-start | bytes 983044
  2.8 10.9 %copy-start.7 = (f32[320]{0:T(512)S(1)}, f32[320]{0:T(512)}, u32[]{:S(2)}) copy-start(f32[320]{0:T(512)} %param.13) | copy-start | bytes 3844
  2.8 10.9 %copy-start.8 = (f32[320]{0:T(512)S(1)}, f32[320]{0:T(512)}, u32[]{:S(2)}) copy-start(f32[320]{0:T(512)} %param.15) | copy-start | bytes 3844
  2.8 11.7 %copy-start.4 = (f32[31,320]{1,0:T(8,128)S(1)}, f32[31,320]{1,0:T(8,128)}, u32[]{:S(2)}) copy-start(f32[31,320]{1,0:T(8,128)} %taps_ref.1) | copy-start | bytes 119044
  2.8 28.8 %all-to-all-start = ((bf16[4,320,512]{2,1,0:T(8,128)(2,1)}), bf16[4,320,512]{2,1,0:T(8,128)(2,1)S(1)}, u32[]{:S(2)}, u32[]{:S(2)}) async-start(bf16[4,320,512]{2,1,0:T(8,128)(2,1)} %shard_map.104), calls=%async_computation | async-start | bytes 2621440 | tf_op jit(solution)/shard_map/all_to_all | solution.py:312
  7.4 6.3 %collective-permute-start.1 = (bf16[16,320]{1,0:T(8,128)(2,1)S(1)}, bf16[16,320]{1,0:T(8,128)(2,1)S(1)}, u32[]{:S(2)}, u32[]{:S(2)}) collective-permute-start(bf16[16,320]{1,0:T(8,128)(2,1)S(1)} %get-tuple-element.30), channel_id=1, source_target_pairs={{4,8},{12,16},{20,24},{28,32},{36,40},{44,48},{52,56},{60,64},{68,... | collective-permute-start | bytes 30728 | tf_op jit(solution)/shard_map/ppermute | solution.py:48
  11.3 3.1 %collective-permute-start = (bf16[16,320]{1,0:T(8,128)(2,1)S(1)}, bf16[16,320]{1,0:T(8,128)(2,1)S(1)}, u32[]{:S(2)}, u32[]{:S(2)}) collective-permute-start(bf16[16,320]{1,0:T(8,128)(2,1)S(1)} %get-tuple-element.31), channel_id=1, source_target_pairs={{0,4},{4,0},{8,12},{12,8},{16,20},{20,16},{24,28},{28,24},{32,36},... | collective-permute-start | bytes 30728 | tf_op jit(solution)/shard_map/ppermute | solution.py:43
  41.0 19.3 %collective-permute-start.4 = (bf16[640,512]{1,0:T(8,128)(2,1)S(1)}, bf16[640,512]{1,0:T(8,128)(2,1)S(1)}, u32[]{:S(2)}, u32[]{:S(2)}) collective-permute-start(bf16[640,512]{1,0:T(8,128)(2,1)S(1)} %get-tuple-element.16.kv_ref.own_ref), channel_id=1, source_target_pairs={{0,8},{4,12},{8,16},{12,20},{16,24},{20,28},{24,32},{28,36},{32,40... | collective-permute-start | bytes 1966088 | tf_op jit(solution)/shard_map/ppermute | solution.py:61
  44.1 16.2 %collective-permute-start.3 = (bf16[640,512]{1,0:T(8,128)(2,1)S(1)}, bf16[640,512]{1,0:T(8,128)(2,1)S(1)}, u32[]{:S(2)}, u32[]{:S(2)}) collective-permute-start(bf16[640,512]{1,0:T(8,128)(2,1)S(1)} %get-tuple-element.16.kv_ref.own_ref), channel_id=1, source_target_pairs={{8,4},{16,12},{24,20},{32,28},{40,36},{48,44},{56,52},{64,60},{72,... | collective-permute-start | bytes 1966088 | tf_op jit(solution)/shard_map/ppermute | solution.py:52
  45.4 14.9 %collective-permute-start.2 = (bf16[640,512]{1,0:T(8,128)(2,1)S(1)}, bf16[640,512]{1,0:T(8,128)(2,1)S(1)}, u32[]{:S(2)}, u32[]{:S(2)}) collective-permute-start(bf16[640,512]{1,0:T(8,128)(2,1)S(1)} %get-tuple-element.16.kv_ref.own_ref), channel_id=1, source_target_pairs={{0,4},{4,0},{8,12},{12,8},{16,20},{20,16},{24,28},{28,24},{32,36},... | collective-permute-start | bytes 1966088 | tf_op jit(solution)/shard_map/ppermute | solution.py:43
  60.3 7.1 %collective-permute-start.5 = (bf16[640,512]{1,0:T(8,128)(2,1)S(1)}, bf16[640,512]{1,0:T(8,128)(2,1)S(1)}, u32[]{:S(2)}, u32[]{:S(2)}) collective-permute-start(bf16[640,512]{1,0:T(8,128)(2,1)S(1)} %collective-permute-done.4.far_ref), channel_id=1, source_target_pairs={{4,0},{12,8},{20,16},{28,24},{36,32},{44,40},{52,48},{60,56},{68,6... | collective-permute-start | bytes 1966088 | tf_op jit(solution)/shard_map/ppermute | solution.py:56
  67.4 11.5 %copy-start.3 = (bf16[128,320]{0,1:T(8,128)(2,1)S(1)}, bf16[128,320]{0,1:T(8,128)(2,1)}, u32[]{:S(2)}) copy-start(bf16[128,320]{0,1:T(8,128)(2,1)} %param.10) | copy-start | bytes 245764
  67.4 11.5 %copy-start.5 = (s32[4]{0:T(128)S(1)}, s32[4]{0:T(128)}, u32[]{:S(2)}) copy-start(s32[4]{0:T(128)} %start_ref.1) | copy-start | bytes 52
  67.4 11.5 %copy-start.6 = (s32[4]{0:T(128)S(1)}, s32[4]{0:T(128)}, u32[]{:S(2)}) copy-start(s32[4]{0:T(128)} %end_ref.1) | copy-start | bytes 52
  70.3 12.9 %collective-permute-start.8 = (bf16[320,512]{1,0:T(8,128)(2,1)S(1)}, bf16[320,512]{1,0:T(8,128)(2,1)S(1)}, u32[]{:S(2)}, u32[]{:S(2)}) collective-permute-start(bf16[320,512]{1,0:T(8,128)(2,1)S(1)} %shard_map.109.b0_ref), channel_id=1, source_target_pairs={{0,2},{1,3},{2,0},{3,1},{4,6},{5,7},{6,4},{7,5},{8,10},{9,11},{10,... | collective-permute-start | bytes 983048 | tf_op jit(solution)/shard_map/ppermute | solution.py:43
  73.6 16.7 %collective-permute-start.7 = (bf16[320,512]{1,0:T(8,128)(2,1)S(1)}, bf16[320,512]{1,0:T(8,128)(2,1)S(1)}, u32[]{:S(2)}, u32[]{:S(2)}) collective-permute-start(bf16[320,512]{1,0:T(8,128)(2,1)S(1)} %shard_map.109.b0_ref), channel_id=1, source_target_pairs={{0,3},{1,2},{2,1},{3,0},{4,7},{5,6},{6,5},{7,4},{8,11},{9,10},{10,... | collective-permute-start | bytes 983048 | tf_op jit(solution)/shard_map/ppermute | solution.py:43
  76.8 13.6 %collective-permute-start.6 = (bf16[320,512]{1,0:T(8,128)(2,1)S(1)}, bf16[320,512]{1,0:T(8,128)(2,1)S(1)}, u32[]{:S(2)}, u32[]{:S(2)}) collective-permute-start(bf16[320,512]{1,0:T(8,128)(2,1)S(1)} %shard_map.109.b0_ref), channel_id=1, source_target_pairs={{0,1},{1,0},{2,3},{3,2},{4,5},{5,4},{6,7},{7,6},{8,9},{9,8},{10,11... | collective-permute-start | bytes 983048 | tf_op jit(solution)/shard_map/ppermute | solution.py:43
  78.9 11.5 %copy-start = (bf16[1280,320]{0,1:T(8,128)(2,1)S(1)}, bf16[1280,320]{0,1:T(8,128)(2,1)}, u32[]{:S(2)}) copy-start(bf16[1280,320]{0,1:T(8,128)(2,1)} %param.17) | copy-start | bytes 2457604
